TPU v7x, 512 devices: a whole 4x4x16 slice. The times are simulated.
512 devices in a mesh: row: 8 (over y, x_hi), col: 16 (over z), depth: 4 (over x_lo, core).
Axes of the slice: x: 4 (x_hi: 2, x_lo: 2; x = x_hi * 2 + x_lo), y: 4, z: 16, core: 2. Of those that a mesh axis runs over, the one named last changes fastest.
Arguments:
- feats: bfloat16 [65536, 256], P(('row', 'col', 'depth')), may hold values from -6 to 6
- tile_values: bfloat16 [8, 16, 4, 96, 128, 128], P('row', 'col', 'depth'), may hold values from 0.0049743652 to 0.049804688
- tile_rows: int32 [8, 16, 4, 96], P('row', 'col', 'depth'), may hold values from 0 to 15
- tile_cols: int32 [8, 16, 4, 96], P('row', 'col', 'depth'), may hold values from 0 to 31
- tile_count: int32 [8, 16, 4], P('row', 'col', 'depth'), may hold values from 1 to 96, as said below
- weight: bfloat16 [256, 256], replicated, may hold values from -0.375 to 0.375
- cotangent: bfloat16 [65536, 256], P(('row', 'col', 'depth')), may hold values from -6 to 6
Outputs:
- hidden: bfloat16 [65536, 256], P(('row', 'col', 'depth'))
- grad_feats: bfloat16 [65536, 256], P(('row', 'col', 'depth'))
- grad_weight: float32 [256, 256], replicated
Inputs may be any that keep to these rules, and one draw needn't show every extreme that they name: `tile_count`: every cell has at least one live slot; in each grid column j, every cell (i, j, l) with i = j * 8 div 16 (for all l) has all 96 slots live.
All inputs are finite; a program needn't handle non-finite values.
Results may differ from a plain program's by a relative error of at most 0.03.
Values may be sent and summed in bfloat16 or wider, within the bound.
A program may use at most 128 MiB of HBM per device.

v0:
```python
import jax
import jax.numpy as jnp
from jax import lax
from jax.sharding import PartitionSpec as P


def per_device(feats, tile_values, tile_rows, tile_cols, tile_count, weight, cotangent):
    tile_vals = tile_values.reshape(tile_values.shape[3:])
    slot_total = tile_vals.shape[0]
    tile_size = tile_vals.shape[1]
    width = feats.shape[1]
    tile_row = tile_rows.reshape(slot_total)
    tile_col = tile_cols.reshape(slot_total)
    tile_num = tile_count.reshape(())
    row_tiles = lax.axis_size("col")
    col_tiles = lax.axis_size("row") * lax.axis_size("depth")
    slot_live = (lax.iota(jnp.int32, slot_total) < tile_num).astype(jnp.float32)
    row_onehot = (tile_row[:, None] == lax.iota(jnp.int32, row_tiles)[None, :]).astype(
        jnp.float32
    ) * slot_live[:, None]
    column_indicator = (tile_col[:, None] == lax.iota(jnp.int32, col_tiles)[None, :]).astype(
        jnp.float32
    ) * slot_live[:, None]
    gathered = lax.all_gather(feats, ("row", "depth"), axis=0, tiled=True)
    gathered = gathered.reshape(col_tiles, tile_size, width)
    picked = gathered[tile_col]
    products = jnp.einsum("kab,kbf->kaf", tile_vals, picked, preferred_element_type=jnp.float32)
    partial_sum = jnp.einsum("kt,kaf->taf", row_onehot, products, precision=lax.Precision.HIGHEST)
    accumulated_total = lax.psum_scatter(
        partial_sum.astype(jnp.bfloat16), "col", scatter_dimension=0, tiled=True
    ).astype(jnp.float32)
    aggregated = accumulated_total.reshape(tile_size, width).astype(jnp.bfloat16)
    preact = jnp.dot(aggregated, weight, preferred_element_type=jnp.float32)
    sigma = jax.nn.sigmoid(preact)
    hidden = (preact * sigma).astype(jnp.bfloat16)
    derivative_before_activation = (
        cotangent.astype(jnp.float32) * sigma * (1.0 + preact * (1.0 - sigma))
    ).astype(jnp.bfloat16)
    nodes_all = tile_size * lax.axis_size("row") * lax.axis_size("col") * lax.axis_size("depth")
    local_weight = jnp.einsum(
        "nf,ng->fg", aggregated, derivative_before_activation, preferred_element_type=jnp.float32
    )
    grad_weight = lax.psum(local_weight, ("row", "col", "depth")) * nodes_all ** (-0.5)
    grad_agg = jnp.einsum(
        "ng,fg->nf", derivative_before_activation, weight, preferred_element_type=jnp.float32
    ).astype(jnp.bfloat16)
    agg_rows = lax.all_gather(grad_agg, "col", axis=0, tiled=True).reshape(
        row_tiles, tile_size, width
    )
    fetched = agg_rows[tile_row]
    contribution = jnp.einsum(
        "kab,kaf->kbf", tile_vals, fetched, preferred_element_type=jnp.float32
    )
    vertical_partial_terms = jnp.einsum(
        "an,arp->nrp", column_indicator, contribution, precision=lax.Precision.HIGHEST
    )
    backward_pass = lax.psum_scatter(
        vertical_partial_terms.astype(jnp.bfloat16),
        ("row", "depth"),
        scatter_dimension=0,
        tiled=True,
    ).astype(jnp.float32)
    grad_feats = backward_pass.reshape(tile_size, width).astype(jnp.bfloat16)
    return (hidden, grad_feats, grad_weight)


def solution(mesh):
    return jax.shard_map(
        per_device,
        mesh=mesh,
        in_specs=(
            P(("row", "col", "depth"), None),
            P("row", "col", "depth", None, None, None),
            P("row", "col", "depth", None),
            P("row", "col", "depth", None),
            P("row", "col", "depth"),
            P(),
            P(("row", "col", "depth"), None),
        ),
        out_specs=(P(("row", "col", "depth"), None), P(("row", "col", "depth"), None), P()),
        check_vma=False,
    )
```

profile of v0, /device:TPU:1, one launch (start us, length us, event | category | flops | bytes accessed | tf_op | source)
XLA Modules:
  0.0 824.9 jit_solution(13770148772941029676)
XLA Ops:
  7.2 0.0 copy-start
  7.2 0.0 all-gather.3.cloned.1.call-start
  7.2 0.7 all-gather.3.cloned.1.call-update
  7.9 0.0 reduce-scatter.3.cloned.1.call-start
  8.8 0.7 fusion.16
  9.4 66.6 %all-gather.3.cloned.1.call-done = bf16[4096,256]{1,0:T(8,128)(2,1)} async-done(((bf16[128,256]{1,0:T(8,128)(2,1)}), bf16[4096,256]{1,0:T(8,128)(2,1)}) %all-gather.3.cloned.1.call-update) | async-done | bytes 2097168 | tf_op jit(solution)/shard_map/all_gather | solution.py:24
  76.1 7.5 gather_fusion
  83.6 0.0 copy-done
  83.6 9.2 %convolution_bitcast_fusion.1 = f32[96,128,256]{1,2,0:T(8,128)} fusion(bf16[96,128,256]{2,1,0:T(8,128)(2,1)} %gather_fusion, bf16[1,1,1,96,128,128]{5,4,3,2,1,0:T(8,128)(2,1)S(1)} %copy-done), kind=kOutput, calls=%fused_computation.3 | convolution fusion | flops 805306368 | bytes 22020096 | tf_op jit(solution)/shard_map/kab,kbf->kaf/dot_general | solution.py:27
  92.7 0.0 copy-start.1
  92.7 12.7 %copy.15 = f32[96,128,256]{2,0,1:T(8,128)} copy(f32[96,128,256]{1,2,0:T(8,128)} %convolution_bitcast_fusion.1) | data formatting | bytes 25165824 | tf_op jit(solution)/shard_map/kab,kbf->kaf/dot_general | solution.py:27
  105.5 0.0 copy-done.1
  105.5 0.0 copy-start.3
  105.5 0.0 copy-start.4
  105.5 8.6 %convolution_convert_fusion.1 = bf16[16,128,256]{2,0,1:T(8,128)(2,1)S(1)} fusion(f32[96,128,256]{2,0,1:T(8,128)} %copy.15, f32[96]{0:T(128)S(1)} %compare_convert_fusion, s32[96]{0:T(128)S(1)} %bitcast.45), kind=kOutput, calls=%fused_computation.7 | convolution fusion | flops 604507136 | bytes 13632256 | tf_op jit(solution)/shard_map/kt,kaf->taf/dot_general | solution.py:28
  114.1 1.3 copy.16
  115.4 0.0 reduce-scatter.3.cloned.1.call-update
  115.4 0.0 all-gather.5.cloned.1.call-start
  115.5 59.5 %reduce-scatter.3.cloned.1.call-done = bf16[1,128,256]{2,1,0:T(8,128)(2,1)} async-done(((bf16[16,128,256]{2,1,0:T(8,128)(2,1)}), bf16[1,128,256]{2,1,0:T(8,128)(2,1)}) %reduce-scatter.3.cloned.1.call-update) | async-done | bytes 65552 | tf_op jit(solution)/shard_map/reduce_scatter | solution.py:29
  175.0 0.0 copy-done.3
  175.0 1.7 multiply_convert_fusion.1
  176.7 0.0 copy-done.4
  176.7 0.8 convolution_convert_fusion.2
  177.5 0.0 all-gather.5.cloned.1.call-update
  177.5 0.0 all-reduce.2.cloned.1.call-start
  177.6 1.8 fusion.2
  179.4 0.0 all-reduce.2.cloned.1.call-update
  179.4 0.2 reduce-scatter.5.cloned.1.call-start
  179.6 67.5 %all-gather.5.cloned.1.call-done = bf16[2048,256]{1,0:T(8,128)(2,1)} async-done(((bf16[128,256]{1,0:T(8,128)(2,1)}), bf16[2048,256]{1,0:T(8,128)(2,1)}) %all-gather.5.cloned.1.call-update) | async-done | bytes 1048592 | tf_op jit(solution)/shard_map/all_gather | solution.py:47
  247.1 7.1 gather_fusion.1
  254.2 9.2 %convolution_bitcast_fusion = f32[96,128,256]{1,2,0:T(8,128)} fusion(bf16[96,128,256]{2,1,0:T(8,128)(2,1)} %gather_fusion.1, bf16[1,1,1,96,128,128]{5,4,3,2,1,0:T(8,128)(2,1)S(1)} %copy-done), kind=kOutput, calls=%fused_computation.2 | convolution fusion | flops 805306368 | bytes 22020096 | tf_op jit(solution)/shard_map/kab,kaf->kbf/dot_general | solution.py:51
  263.4 0.0 copy-start.2
  263.4 12.7 %copy.18 = f32[96,128,256]{2,0,1:T(8,128)} copy(f32[96,128,256]{1,2,0:T(8,128)} %convolution_bitcast_fusion) | data formatting | bytes 25165824 | tf_op jit(solution)/shard_map/kab,kaf->kbf/dot_general | solution.py:51
  276.1 0.0 copy-done.2
  276.1 9.0 %convolution_convert_fusion = bf16[32,128,256]{2,0,1:T(8,128)(2,1)S(1)} fusion(f32[96,128,256]{2,0,1:T(8,128)} %copy.18, f32[96]{0:T(128)S(1)} %compare_convert_fusion, s32[96]{0:T(128)S(1)} %bitcast.46), kind=kOutput, calls=%fused_computation.6 | convolution fusion | flops 1209014272 | bytes 14680832 | tf_op jit(solution)/shard_map/an,arp->nrp/dot_general | solution.py:54
  285.1 2.5 copy.19
  287.7 0.0 reduce-scatter.5.cloned.1.call-update
  287.7 428.5 %all-reduce.2.cloned.1.call-done = f32[256,256]{1,0:T(8,128)} async-done(((f32[256,256]{1,0:T(8,128)}), f32[256,256]{1,0:T(8,128)}) %all-reduce.2.cloned.1.call-update) | async-done | bytes 262160 | tf_op jit(solution)/shard_map/psum | solution.py:43
  716.2 1.7 broadcast_multiply_fusion
  717.9 100.5 %reduce-scatter.5.cloned.1.call-done = bf16[1,128,256]{2,1,0:T(8,128)(2,1)} async-done(((bf16[32,128,256]{2,1,0:T(8,128)(2,1)}), bf16[1,128,256]{2,1,0:T(8,128)(2,1)}) %reduce-scatter.5.cloned.1.call-update) | async-done | bytes 65552 | tf_op jit(solution)/shard_map/reduce_scatter | solution.py:57
  (4 shorter events, 0.0 us)
Async XLA Ops:
  7.2 76.4 %copy-start = (bf16[1,1,1,96,128,128]{5,4,3,2,1,0:T(8,128)(2,1)S(1)}, bf16[1,1,1,96,128,128]{5,4,3,2,1,0:T(8,128)(2,1)}, u32[]{:S(2)}) copy-start(bf16[1,1,1,96,128,128]{5,4,3,2,1,0:T(8,128)(2,1)} %param.8) | copy-start | bytes 9437188
  7.2 68.9 %all-gather.3.cloned.1.call-start = ((), (), s32[]{:S(2)}) async-start(), calls=%async_computation.2 | async-start | bytes 2162688 | tf_op jit(solution)/shard_map/all_gather | solution.py:24
  7.9 167.1 %reduce-scatter.3.cloned.1.call-start = ((), (), s32[]{:S(2)}) async-start(), calls=%async_computation.3 | async-start | bytes 1114112 | tf_op jit(solution)/shard_map/reduce_scatter | solution.py:29
  92.7 12.7 %copy-start.1 = (s32[1,1,1,96]{3,2,1,0:T(1,128)S(1)}, s32[1,1,1,96]{3,2,1,0:T(1,128)}, u32[]{:S(2)}) copy-start(s32[1,1,1,96]{3,2,1,0:T(1,128)} %param.9) | copy-start | bytes 1156
  105.5 69.5 %copy-start.3 = (bf16[256,256]{1,0:T(8,128)(2,1)S(1)}, bf16[256,256]{1,0:T(8,128)(2,1)}, u32[]{:S(2)}) copy-start(bf16[256,256]{1,0:T(8,128)(2,1)} %param.12) | copy-start | bytes 393220
  105.5 71.2 %copy-start.4 = (bf16[128,256]{1,0:T(8,128)(2,1)S(1)}, bf16[128,256]{1,0:T(8,128)(2,1)}, u32[]{:S(2)}) copy-start(bf16[128,256]{1,0:T(8,128)(2,1)} %param.13) | copy-start | bytes 196612
  115.4 131.7 %all-gather.5.cloned.1.call-start = ((), (), s32[]{:S(2)}) async-start(), calls=%async_computation.4 | async-start | bytes 1114112 | tf_op jit(solution)/shard_map/all_gather | solution.py:47
  177.5 538.7 %all-reduce.2.cloned.1.call-start = ((), (), s32[]{:S(2)}) async-start(), calls=%async_computation.6 | async-start | bytes 524288 | tf_op jit(solution)/shard_map/psum | solution.py:43
  179.4 639.0 %reduce-scatter.5.cloned.1.call-start = ((), (), s32[]{:S(2)}) async-start(), calls=%async_computation.5 | async-start | bytes 2162688 | tf_op jit(solution)/shard_map/reduce_scatter | solution.py:57
  263.4 12.7 %copy-start.2 = (s32[1,1,1,96]{3,2,1,0:T(1,128)S(1)}, s32[1,1,1,96]{3,2,1,0:T(1,128)}, u32[]{:S(2)}) copy-start(s32[1,1,1,96]{3,2,1,0:T(1,128)} %param.10) | copy-start | bytes 1156
Sparse Core Ops, SparseCore 0:
  11.1 64.8 all-gather.2
  115.5 59.4 reduce-scatter.2
  177.9 69.2 all-gather.4
  253.9 462.2 all-reduce.1
  721.1 97.3 reduce-scatter.4
where the time goes:
time: 826 us; the launch traced here: 825 us
  waiting for transfers between devices  723 us (88%)
  local copies, waits for them, and re-layouts  44 us (5%)
  matrix products  40.2 us (5%)
  between operations  14.6 us (2%)
    psum x1, waiting for transfers between devices, per_device(): lax.psum(local_weight, ('row', 'col', 'depth')) * nodes_all ** (-0.5)  429 us
    reduce_scatter x1, waiting for transfers between devices, per_device(): lax.psum_scatter(vertical_partial_terms.astype(jnp.bfloat16), ('row', 'de...  101 us
    all_gather x1, waiting for transfers between devices, per_device(): lax.all_gather(grad_agg, 'col', axis=0, tiled=True)  67.5 us
    all_gather x1, waiting for transfers between devices, per_device(): gathered = lax.all_gather(feats, ('row', 'depth'), axis=0, tiled=True)  66.6 us
    reduce_scatter x1, waiting for transfers between devices, per_device(): lax.psum_scatter(partial_sum.astype(jnp.bfloat16), 'col', scatter_dimensi...  59.5 us
  transfers between devices with their start and end apart: 5, of which 5 were waited for; matrix products, arithmetic and copies ran while one was open for 5% of the time, Pallas kernels for 0%

commit v1 on v0

v1 whole, which is shorter than its diff:
```python
import jax
import jax.numpy as jnp
from jax import lax
from jax.experimental import pallas as pl
from jax.experimental.pallas import tpu as pltpu
from jax.sharding import PartitionSpec as P

MESH = pl.DeviceIdType.MESH
BF, F32 = jnp.bfloat16, jnp.float32

NX, NY, NZ = 4, 4, 16
TILE, F, SLOTS = 128, 256, 96
NROWS, NCOLS = NZ, NX * NY * 2
FPOS, BPOS = SLOTS + NROWS, SLOTS + NCOLS
FPAIRS, BPAIRS = FPOS // 2, BPOS // 2
Q = 4
REL = (2, 1, 3, 0)

F_IDX, F_OTH = 0, FPOS
F_KEEP = F_OTH + FPOS
F_LAST = F_KEEP + FPAIRS
B_IDX = F_LAST + NROWS
B_OTH = B_IDX + BPOS
B_KEEP = B_OTH + BPOS
B_LAST = B_KEEP + BPAIRS
TABLE = B_LAST + NCOLS


def schedule(key, other, live, keys, other_zero):
    slots = key.shape[0]
    positions = slots + keys
    hot = (key[:, None] == lax.iota(jnp.int32, keys)[None, :]) & live[:, None]
    hot_i = hot.astype(jnp.int32)
    count = jnp.sum(hot_i, axis=0)
    padded = (count + 1) // 2 * 2
    before = lax.iota(jnp.int32, keys)[:, None] < lax.iota(jnp.int32, keys)[None, :]
    start = jnp.sum(jnp.where(before, padded[:, None], 0), axis=0)
    earlier = lax.iota(jnp.int32, slots)[:, None] < lax.iota(jnp.int32, slots)[None, :]
    same = (key[:, None] == key[None, :]) & live[:, None] & earlier
    rank = jnp.sum(same.astype(jnp.int32), axis=0)
    place = jnp.sum(hot_i * start[None, :], axis=1) + rank
    at = (place[:, None] == lax.iota(jnp.int32, positions)[None, :]) & live[:, None]
    slot = jnp.sum(jnp.where(at, lax.iota(jnp.int32, slots)[:, None], 0), axis=0)
    partner = jnp.sum(jnp.where(at, other[:, None] - other_zero, 0), axis=0) + other_zero
    pairs = positions // 2
    opens = (start[:, None] == 2 * lax.iota(jnp.int32, pairs)[None, :]) & (count > 0)[:, None]
    keep = 1 - jnp.sum(opens.astype(jnp.int32), axis=0)
    last = jnp.where(count > 0, (start + padded) // 2 - 1, pairs)
    return [slot, partner, keep, last]


def wait(ref, sem):
    pltpu.make_async_copy(ref, ref, sem).wait()


def kernel(
    table, feats, tiles, weight, cot, hidden_o, gf_o, gw_o,
    av, xg, fout, acc, wv, cv, zs, zr, gt, bout, sib_s, sib_r,
    d2s, d2r, d1s, d1r, vv, e2s, e2r, e1s, e1r, gft, gfv, hv,
    w1s, w1r, w2s, w2r, w3s, w3r, w4, w5, w6, w7, w8, lw, gwv,
    loc, ag_send, ag_recv, zs_send, zs_recv, zg_send, zg_recv,
    sb_send, sb_recv, rp_send, rp_recv, w_send, w_recv, out_sem,
):
    row, z, depth = lax.axis_index("row"), lax.axis_index("col"), lax.axis_index("depth")
    y, x, core = row // 2, (row % 2) * 2 + depth // 2, depth % 2

    def dev(dx=0, dy=0, dz=0, flip=0, zz=None):
        nx, ny = (x + dx) % NX, (y + dy) % NY
        nz = (z + dz + NZ) % NZ if zz is None else zz
        nc = (core + flip) % 2
        return {"row": ny * 2 + nx // 2, "col": nz, "depth": (nx % 2) * 2 + nc}

    def send(src, dst, ssem, rsem, to):
        pltpu.make_async_remote_copy(
            src_ref=src, dst_ref=dst, send_sem=ssem, recv_sem=rsem, device_id=to, device_id_type=MESH
        ).start()

    zi, zq = z % 4, z // 4
    partners = [dev(flip=1), dev(dz=1), dev(dz=-1)]
    for k in (1, 2, 3):
        partners += [dev(dx=k), dev(dy=k), dev(dz=4 * k), dev(zz=zq * 4 + (zi + k) % 4)]

    mine = 8 * y + 2 * x + core
    own_copy = pltpu.make_async_copy(feats, xg.at[mine], loc.at[0])
    own_copy.start()
    tile_copy = pltpu.make_async_copy(tiles, av, loc.at[1])
    tile_copy.start()
    weight_copy = pltpu.make_async_copy(weight, wv, loc.at[2])
    weight_copy.start()
    cot_copy = pltpu.make_async_copy(cot, cv, loc.at[3])
    cot_copy.start()

    barrier = pltpu.get_barrier_semaphore()
    for to in partners:
        pl.semaphore_signal(barrier, inc=1, device_id=to, device_id_type=MESH)
    pl.semaphore_wait(barrier, len(partners))

    xg[NCOLS] = jnp.zeros((TILE, F), BF)
    gt[NZ] = jnp.zeros((F, TILE), BF)
    fout[FPAIRS] = jnp.zeros((TILE, F), BF)
    bout[BPAIRS] = jnp.zeros((F, TILE), BF)

    def to_ab(h, da, db):
        return dev(dx=da, dy=db) if h == 0 else dev(dx=db, dy=da)

    def piece(h, da, db, flip=0):
        dx, dy = (da, db) if h == 0 else (db, da)
        return 8 * ((y + dy) % NY) + 2 * ((x + dx) % NX) + (core + flip) % 2

    def rows(h, part):
        if part is None:
            return pl.ds(64 * h, 64)
        return pl.ds(64 * h + 32 * part, 32)

    def xpart(h, da, db, part=None, flip=0):
        return xg.at[piece(h, da, db, flip), rows(h, part)]

    def forward(h, da, db, part, to, k, own=False):
        src = feats.at[rows(h, part)] if own else xpart(h, da, db, part)
        send(src, xpart(h, da, db, part), ag_send, ag_recv.at[h, k], to)

    def to_b(h, e, own=False):
        forward(h, e, 0, None, to_ab(h, 0, 1), 4 + e, own)
        forward(h, e, 0, None, to_ab(h, 0, 3), 8 + e, own)

    def to_sib(h, da, db, own=False):
        forward(h, da, db, None, dev(flip=1), 20 + 4 * da + db, own)

    for h in (0, 1):
        forward(h, 0, 0, None, to_ab(h, 1, 0), 0, True)
        forward(h, 0, 0, None, to_ab(h, 3, 0), 1, True)
    for h in (0, 1):
        to_b(h, 0, True)
        to_sib(h, 0, 0, True)
    for h in (0, 1):
        wait(xpart(h, 3, 0), ag_recv.at[h, 0])
        forward(h, 3, 0, 0, to_ab(h, 1, 0), 2)
        to_b(h, 3)
        wait(xpart(h, 1, 0), ag_recv.at[h, 1])
        forward(h, 1, 0, 1, to_ab(h, 3, 0), 3)
        to_b(h, 1)
        to_sib(h, 3, 0)
        to_sib(h, 1, 0)
    for h in (0, 1):
        wait(xpart(h, 2, 0, 0), ag_recv.at[h, 2])
        wait(xpart(h, 2, 0, 1), ag_recv.at[h, 3])
        to_b(h, 2)
        to_sib(h, 2, 0)
    for e in (0, 3, 1, 2):
        for h in (0, 1):
            wait(xpart(h, e, 3), ag_recv.at[h, 4 + e])
            forward(h, e, 3, 0, to_ab(h, 0, 1), 12 + e)
            wait(xpart(h, e, 1), ag_recv.at[h, 8 + e])
            forward(h, e, 1, 1, to_ab(h, 0, 3), 16 + e)
            to_sib(h, e, 3)
            to_sib(h, e, 1)
    for e in (0, 3, 1, 2):
        for h in (0, 1):
            wait(xpart(h, e, 2, 0), ag_recv.at[h, 12 + e])
            wait(xpart(h, e, 2, 1), ag_recv.at[h, 16 + e])
            to_sib(h, e, 2)
    for h in (0, 1):
        for da in range(4):
            for db in range(4):
                wait(xpart(h, da, db, None, 1), ag_recv.at[h, 20 + 4 * da + db])
    own_copy.wait()
    tile_copy.wait()
    weight_copy.wait()
    cot_copy.wait()

    acc[...] = jnp.zeros_like(acc)

    def forward_pair(q, carry):
        a = jnp.concatenate([av[table[F_IDX + 2 * q]], av[table[F_IDX + 2 * q + 1]]], axis=1)
        b = jnp.concatenate([xg[table[F_OTH + 2 * q]], xg[table[F_OTH + 2 * q + 1]]], axis=0)
        keep = table[F_KEEP + q].astype(F32)
        total = acc[...] * keep + jnp.dot(a, b, preferred_element_type=F32)
        acc[...] = total
        fout[q] = total.astype(BF)
        return carry

    lax.fori_loop(0, FPAIRS, forward_pair, 0, unroll=4)

    ROWS = TILE // Q

    def hops(d, q):
        return 8 if (d == 0) == (q % 2 == 0) else 7

    def zto(d):
        return dev(dz=1 if d == 0 else -1)

    def zrow(d, q, m):
        dist = hops(d, q) - m
        return (z + dist) % NZ if d == 0 else (z - dist + NZ) % NZ

    def sum_hop(m, first, final):
        for q in range(Q):
            part = pl.ds(q * ROWS, ROWS)
            for d in (0, 1):
                if final and hops(d, q) == 7:
                    continue
                term = fout[table[F_LAST + zrow(d, q, m)], part, :]
                if not first:
                    wait(zr.at[d, m - 1, part], zs_recv.at[d, m - 1, q])
                    term = (term.astype(F32) + zr[d, m - 1, part, :].astype(F32)).astype(BF)
                zs[d, m, part, :] = term
                send(zs.at[d, m, part], zr.at[d, m, part], zs_send, zs_recv.at[d, m, q], zto(d))

    sum_hop(0, True, False)

    def sum_step(m, carry):
        sum_hop(m, False, False)
        return carry

    lax.fori_loop(1, 7, sum_step, 0)
    sum_hop(7, False, True)
    totals = []
    for q in range(Q):
        part = pl.ds(q * ROWS, ROWS)
        total = fout[table[F_LAST + z], part, :].astype(F32)
        for d in (0, 1):
            m = hops(d, q) - 1
            wait(zr.at[d, m, part], zs_recv.at[d, m, q])
            total = total + zr[d, m, part, :].astype(F32)
        totals.append(total.astype(BF))
    agg = jnp.concatenate(totals, axis=0)

    w = wv[...]
    pre = jnp.dot(agg, w, preferred_element_type=F32)
    sig = jax.nn.sigmoid(pre)
    grad_pre = (cv[...].astype(F32) * sig * (1.0 + pre * (1.0 - sig))).astype(BF)
    gt[z] = lax.dot_general(w, grad_pre, (((1,), (1,)), ((), ())), preferred_element_type=F32).astype(BF)

    FR = F // Q

    def zpiece(d, m):
        return (z - m + NZ) % NZ if d == 0 else (z + m) % NZ

    def gather_hop(m):
        for q in range(Q):
            part = pl.ds(q * FR, FR)
            for d in (0, 1):
                ref = gt.at[zpiece(d, m), part]
                if m > 0:
                    wait(ref, zg_recv.at[d, m - 1, q])
                if m < hops(d, q):
                    send(ref, ref, zg_send, zg_recv.at[d, m, q], zto(d))

    gather_hop(0)
    hv[...] = (pre * sig).astype(BF)
    hidden_copy = pltpu.make_async_copy(hv, hidden_o, out_sem.at[0])
    hidden_copy.start()
    lw[...] = lax.dot_general(agg, grad_pre, (((0,), (0,)), ((), ())), preferred_element_type=F32)
    for k in range(4):
        w1s[k] = lw[pl.ds(64 * k, 64), :].astype(BF)

    def w_stage1():
        for k in (1, 2, 3):
            send(w1s.at[(y + k) % NY], w1r.at[k - 1], w_send.at[0], w_recv.at[0], dev(dy=k))

    def w_stage2():
        wait(w1r, w_recv.at[0])
        total = lw[pl.ds(pl.multiple_of(64 * y, 64), 64), :]
        for k in range(3):
            total = total + w1r[k].astype(F32)
        for k in range(4):
            w2s[k] = total[16 * k : 16 * k + 16, :].astype(BF)
        for k in (1, 2, 3):
            send(w2s.at[(x + k) % NX], w2r.at[k - 1], w_send.at[1], w_recv.at[1], dev(dx=k))

    def w_stage3():
        wait(w2r, w_recv.at[1])
        total = w2s[x].astype(F32)
        for k in range(3):
            total = total + w2r[k].astype(F32)
        w3s[0] = total[:, :128].astype(BF)
        w3s[1] = total[:, 128:].astype(BF)
        send(w3s.at[1 - core], w3r, w_send.at[2], w_recv.at[2], dev(flip=1))

    def w_stage4():
        wait(w3r, w_recv.at[2])
        w4[zi] = (w3s[core].astype(F32) + w3r[...].astype(F32)).astype(BF)
        for k in (1, 2, 3):
            send(w4.at[zi], w4.at[zi], w_send.at[3], w_recv.at[3], dev(zz=zq * 4 + (zi + k) % 4))

    def sum4(ref):
        total = ref[0].astype(F32)
        for k in (1, 2, 3):
            total = total + ref[k].astype(F32)
        return total.astype(BF)

    def w_stage5():
        wait(w4.at[pl.ds(0, 3)], w_recv.at[3])
        w5[zq] = sum4(w4)
        for k in (1, 2, 3):
            send(w5.at[zq], w5.at[zq], w_send.at[4], w_recv.at[4], dev(dz=4 * k))

    def w_stage6():
        wait(w5.at[pl.ds(0, 3)], w_recv.at[4])
        w6[core] = sum4(w5)
        send(w6.at[core], w6.at[core], w_send.at[5], w_recv.at[5], dev(flip=1))

    def w_stage7():
        wait(w6.at[0], w_recv.at[5])
        w7[x] = w6[...]
        for k in (1, 2, 3):
            send(w7.at[x], w7.at[x], w_send.at[6], w_recv.at[6], dev(dx=k))

    def w_stage8():
        wait(w7.at[pl.ds(0, 3)], w_recv.at[6])
        w8[y] = w7[...]
        for k in (1, 2, 3):
            send(w8.at[y], w8.at[y], w_send.at[7], w_recv.at[7], dev(dy=k))

    def w_stage9():
        wait(w8.at[pl.ds(0, 3)], w_recv.at[7])
        for i in range(4):
            for j in range(4):
                for k in range(2):
                    gwv[pl.ds(64 * i + 16 * j, 16), pl.ds(128 * k, 128)] = w8[i, j, k].astype(F32)
        gw_copy = pltpu.make_async_copy(gwv, gw_o, out_sem.at[1])
        gw_copy.start()
        return gw_copy

    w_stage1()
    for m in range(1, 9):
        for q in range(Q):
            part = pl.ds(q * FR, FR)
            for d in (0, 1):
                if m > hops(d, q):
                    continue
                ref = gt.at[zpiece(d, m), part]
                wait(ref, zg_recv.at[d, m - 1, q])
                if m < hops(d, q):
                    send(ref, ref, zg_send, zg_recv.at[d, m, q], zto(d))
        if m == 3:
            w_stage2()
        if m == 5:
            w_stage3()
        if m == 7:
            w_stage4()

    w_stage5()

    def backward_pair(q, carry):
        a = jnp.concatenate([gt[table[B_OTH + 2 * q]], gt[table[B_OTH + 2 * q + 1]]], axis=1)
        b = jnp.concatenate([av[table[B_IDX + 2 * q]], av[table[B_IDX + 2 * q + 1]]], axis=0)
        keep = table[B_KEEP + q].astype(F32)
        total = gfv[...] * keep + jnp.dot(a, b, preferred_element_type=F32)
        gfv[...] = total
        bout[q] = total.astype(BF)
        return carry

    gfv[...] = jnp.zeros_like(gfv)
    lax.fori_loop(0, BPAIRS // 2, backward_pair, 0, unroll=4)
    w_stage6()
    lax.fori_loop(BPAIRS // 2, BPAIRS, backward_pair, 0, unroll=4)
    w_stage7()

    def term(h, g, e, flip=0):
        dx, dy = (e, g) if h == 0 else (g, e)
        c = 8 * ((y + dy) % NY) + 2 * ((x + dx) % NX) + (core + flip) % 2
        return bout[table[B_LAST + c], pl.ds(128 * h, 128), :]

    def to_h(h, da, db):
        return dev(dx=db, dy=da) if h == 0 else dev(dx=da, dy=db)

    for g in range(4):
        for h in (0, 1):
            for e in range(4):
                sib_s[h, g, e] = term(h, REL[g], REL[e], 1)
            send(sib_s.at[h, g], sib_r.at[h, g], sb_send, sb_recv.at[h, g], dev(flip=1))

    def both(h, g, e):
        return term(h, REL[g], REL[e]).astype(F32) + sib_r[h, g, e].astype(F32)

    for h in (0, 1):
        wait(sib_r.at[h, 0], sb_recv.at[h, 0])
        for e in range(4):
            total = both(h, 0, e).astype(BF)
            d2s[h, 0, e] = total[:64]
            d2s[h, 1, e] = total[64:]
        send(d2s.at[h, 0], d2r.at[h, 0], rp_send.at[0], rp_recv.at[h, 0], to_h(h, 1, 0))
        send(d2s.at[h, 1], d2r.at[h, 1], rp_send.at[0], rp_recv.at[h, 1], to_h(h, 3, 0))
    for h in (0, 1):
        for d in (0, 1):
            wait(sib_r.at[h, 1 + d], sb_recv.at[h, 1 + d])
            wait(d2r.at[h, d], rp_recv.at[h, d])
            for e in range(4):
                total = both(h, 1 + d, e)
                got = d2r[h, d, e].astype(F32)
                if d == 0:
                    total = jnp.concatenate([total[:64] + got, total[64:]], axis=0)
                else:
                    total = jnp.concatenate([total[:64], total[64:] + got], axis=0)
                d1s[h, d, e] = total.astype(BF)
            send(d1s.at[h, d], d1r.at[h, d], rp_send.at[1], rp_recv.at[h, 2 + d], to_h(h, 1 + 2 * d, 0))
    w_stage8()
    for h in (0, 1):
        wait(sib_r.at[h, 3], sb_recv.at[h, 3])
        for d in (0, 1):
            wait(d1r.at[h, d], rp_recv.at[h, 2 + d])
        for e in range(4):
            vv[h, e] = both(h, 3, e) + d1r[h, 0, e].astype(F32) + d1r[h, 1, e].astype(F32)
            if e == 0:
                total = vv[h, 0].astype(BF)
                e2s[h, 0] = total[:64]
                e2s[h, 1] = total[64:]
                send(e2s.at[h, 0], e2r.at[h, 0], rp_send.at[2], rp_recv.at[h, 4], to_h(h, 0, 1))
                send(e2s.at[h, 1], e2r.at[h, 1], rp_send.at[2], rp_recv.at[h, 5], to_h(h, 0, 3))
    for h in (0, 1):
        for d in (0, 1):
            wait(e2r.at[h, d], rp_recv.at[h, 4 + d])
            total = vv[h, 1 + d]
            got = e2r[h, d].astype(F32)
            if d == 0:
                total = jnp.concatenate([total[:64] + got, total[64:]], axis=0)
            else:
                total = jnp.concatenate([total[:64], total[64:] + got], axis=0)
            e1s[h, d] = total.astype(BF)
            send(e1s.at[h, d], e1r.at[h, d], rp_send.at[3], rp_recv.at[h, 6 + d], to_h(h, 0, 1 + 2 * d))
    gw_copy = w_stage9()
    for h in (0, 1):
        for d in (0, 1):
            wait(e1r.at[h, d], rp_recv.at[h, 6 + d])
        gft[pl.ds(128 * h, 128), :] = vv[h, 3] + e1r[h, 0].astype(F32) + e1r[h, 1].astype(F32)
    hv2 = xg.at[NCOLS]
    hv2[...] = jnp.transpose(gft[...]).astype(BF)
    gf_copy = pltpu.make_async_copy(hv2, gf_o, out_sem.at[2])
    gf_copy.start()

    hidden_copy.wait()
    gw_copy.wait()
    gf_copy.wait()
    wait(xg.at[pl.ds(0, NCOLS - 1)], ag_send)
    wait(xg.at[pl.ds(0, NZ - 1)], zs_send)
    wait(xg.at[pl.ds(0, NZ - 1)], zg_send)
    wait(sib_s, sb_send)
    wait(d2s, rp_send.at[0])
    wait(d1s, rp_send.at[1])
    wait(e2s, rp_send.at[2])
    wait(e1s, rp_send.at[3])
    wait(w1r, w_send.at[0])
    wait(w2r, w_send.at[1])
    wait(w3r, w_send.at[2])
    wait(w4.at[pl.ds(0, 3)], w_send.at[3])
    wait(w5.at[pl.ds(0, 3)], w_send.at[4])
    wait(w6.at[0], w_send.at[5])
    wait(w7.at[pl.ds(0, 3)], w_send.at[6])
    wait(w8.at[pl.ds(0, 3)], w_send.at[7])


def per_device(feats, tile_values, tile_rows, tile_cols, tile_count, weight, cotangent):
    tiles = tile_values.reshape(tile_values.shape[3:])
    tile_row, tile_col = tile_rows.reshape(-1), tile_cols.reshape(-1)
    live = lax.iota(jnp.int32, SLOTS) < tile_count.reshape(())
    table = jnp.concatenate(
        schedule(tile_row, tile_col, live, NROWS, NCOLS) + schedule(tile_col, tile_row, live, NCOLS, NZ)
    )
    vm, dma = pltpu.VMEM, pltpu.SemaphoreType.DMA
    scratch = [
        vm((SLOTS, TILE, TILE), BF),
        vm((NCOLS + 1, TILE, F), BF),
        vm((FPAIRS + 1, TILE, F), BF),
        vm((TILE, F), F32),
        vm((F, F), BF),
        vm((TILE, F), BF),
        vm((2, 8, TILE, F), BF),
        vm((2, 8, TILE, F), BF),
        vm((NZ + 1, F, TILE), BF),
        vm((BPAIRS + 1, F, TILE), BF),
        vm((2, 4, 4, 128, TILE), BF),
        vm((2, 4, 4, 128, TILE), BF),
        vm((2, 2, 4, 64, TILE), BF),
        vm((2, 2, 4, 64, TILE), BF),
        vm((2, 2, 4, 128, TILE), BF),
        vm((2, 2, 4, 128, TILE), BF),
        vm((2, 4, 128, TILE), F32),
        vm((2, 2, 64, TILE), BF),
        vm((2, 2, 64, TILE), BF),
        vm((2, 2, 128, TILE), BF),
        vm((2, 2, 128, TILE), BF),
        vm((F, TILE), F32),
        vm((F, TILE), F32),
        vm((TILE, F), BF),
        vm((4, 64, F), BF),
        vm((3, 64, F), BF),
        vm((4, 16, F), BF),
        vm((3, 16, F), BF),
        vm((2, 16, 128), BF),
        vm((16, 128), BF),
        vm((4, 16, 128), BF),
        vm((4, 16, 128), BF),
        vm((2, 16, 128), BF),
        vm((4, 2, 16, 128), BF),
        vm((4, 4, 2, 16, 128), BF),
        vm((F, F), F32),
        vm((F, F), F32),
        dma((4,)),
        dma,
        dma((2, 36)),
        dma,
        dma((2, 8, Q)),
        dma,
        dma((2, 8, Q)),
        dma,
        dma((2, 4)),
        dma((4,)),
        dma((2, 8)),
        dma((8,)),
        dma((8,)),
        dma((3,)),
    ]
    any_spec = pl.BlockSpec(memory_space=pl.ANY)
    hidden, grad_feats, grad_weight = pl.pallas_call(
        kernel,
        out_shape=(
            jax.ShapeDtypeStruct((TILE, F), BF),
            jax.ShapeDtypeStruct((TILE, F), BF),
            jax.ShapeDtypeStruct((F, F), F32),
        ),
        in_specs=[pl.BlockSpec(memory_space=pltpu.SMEM)] + [any_spec] * 4,
        out_specs=(any_spec,) * 3,
        scratch_shapes=scratch,
        compiler_params=pltpu.CompilerParams(
            collective_id=0, has_side_effects=True, vmem_limit_bytes=40 * 1024 * 1024
        ),
        cost_estimate=pl.CostEstimate(flops=2_000_000_000, bytes_accessed=4_000_000, transcendentals=32768),
    )(table, feats, tiles, weight, cotangent)
    nodes = TILE * NX * NY * NZ * 2
    return hidden, grad_feats, grad_weight * nodes ** (-0.5)


def solution(mesh):
    return jax.shard_map(
        per_device,
        mesh=mesh,
        in_specs=(
            P(("row", "col", "depth"), None),
            P("row", "col", "depth", None, None, None),
            P("row", "col", "depth", None),
            P("row", "col", "depth", None),
            P("row", "col", "depth"),
            P(),
            P(("row", "col", "depth"), None),
        ),
        out_specs=(P(("row", "col", "depth"), None), P(("row", "col", "depth"), None), P()),
        check_vma=False,
    )
```

time: 826 us -> 132 us (0.16)
  waiting for transfers between devices: 723 us -> 0 us
  Pallas kernels: 0 us -> 117 us
  matrix products: 40.2 us -> 0 us
  local copies, waits for them, and re-layouts: 44 us -> 5.81 us
  between operations: 14.6 us -> 1.36 us
    psum x1 -> x0, waiting for transfers between devices: 429 us -> none  [per_device(): lax.psum(local_weight, ('row', 'col', 'depth')) * nodes_all ** (-0.5)]
    reduce_scatter x2 -> x0, waiting for transfers between devices: 160 us -> none  [the longest x1 101 us: per_device(): lax.psum_scatter(vertical_partial_terms.astype(jnp.bfloat16), ('row', 'de...]
    all_gather x2 -> x0, waiting for transfers between devices: 134 us -> none  [the longest x1 67.5 us: per_device(): lax.all_gather(grad_agg, 'col', axis=0, tiled=True)]
    pallas_call x0 -> x1, Pallas kernels: none -> 117 us  [per_device(): pl.pallas_call(kernel, out_shape=(jax.ShapeDtypeStruct((TILE, F), BF), ja...]
    dot_general x7 -> x0, matrix products: 40.2 us -> none  [the longest x1 9.15 us: per_device(): jnp.einsum('kab,kbf->kaf', tile_vals, picked, preferred_element_type=jnp....]
    dot_general x2 -> x0, local copies, waits for them, and re-layouts: 25.4 us -> none  [the longest x1 12.7 us: per_device(): jnp.einsum('kab,kbf->kaf', tile_vals, picked, preferred_element_type=jnp....]
    gather x2 -> x0, local copies, waits for them, and re-layouts: 14.7 us -> none  [the longest x1 7.53 us: per_device(): picked = gathered[tile_col]]
  transfers between devices with their start and end apart: 5 -> 0, of which waited for: 5 -> 0; matrix products, arithmetic and copies ran while one was open for 5% -> 0% of each run, Pallas kernels for 0% -> 0%
where the time goes in v1:
time: 132 us; the launch traced here: 131 us
  Pallas kernels  117 us (89%)
  other arithmetic  6.65 us (5%)
  local copies, waits for them, and re-layouts  5.81 us (4%)
  between operations  1.36 us (1%)
    pallas_call x1, Pallas kernels, per_device(): pl.pallas_call(kernel, out_shape=(jax.ShapeDtypeStruct((TILE, F), BF), ja...  117 us
    unnamed x10, local copies, waits for them, and re-layouts  5.73 us

profile of v1, /device:TPU:1, one launch (start us, length us, event | category | flops | bytes accessed | tf_op | source)
XLA Modules:
  0.0 131.1 jit_solution(16904309640855036072)
XLA Ops:
  1.3 0.8 convert_reduce_fusion.5
  2.1 0.8 convert_reduce_fusion.3
  2.9 0.1 select_reduce_fusion.5
  3.0 0.7 select_reduce_fusion.4
  3.7 0.1 select_reduce_fusion.7
  3.9 0.7 select_reduce_fusion.6
  4.6 0.7 broadcast_add_fusion.1
  5.3 0.7 broadcast_add_fusion.3
  5.9 0.1 convert_reduce_fusion.4
  6.0 0.1 convert_reduce_fusion.2
  6.1 0.9 convert_reduce_fusion
  7.0 0.1 select_reduce_fusion.2
  7.1 0.1 select_reduce_fusion
  7.3 0.1 concatenate.3.table
  7.4 0.0 copy-start
  7.4 1.9 %copy-done = bf16[1,1,1,96,128,128]{5,4,3,2,1,0:T(8,128)(2,1)S(1)} copy-done((bf16[1,1,1,96,128,128]{5,4,3,2,1,0:T(8,128)(2,1)S(1)}, bf16[1,1,1,96,128,128]{5,4,3,2,1,0:T(8,128)(2,1)}, u32[]{:S(2)}) %copy-start) | copy-done | bytes 3145752
  9.2 0.0 copy-start.1
  9.2 0.9 copy-done.1
  10.2 0.0 copy-start.2
  10.2 0.8 copy-done.2
  11.0 0.0 copy-start.3
  11.0 0.8 copy-done.3
  11.8 117.2 %shard_map.94 = (bf16[128,256]{1,0:T(8,128)(2,1)S(1)}, bf16[128,256]{1,0:T(8,128)(2,1)S(1)}, f32[256,256]{1,0:T(8,128)S(1)}) custom-call(s32[648]{0:T(1024)S(1)} %concatenate.3.table, bf16[128,256]{1,0:T(8,128)(2,1)S(1)} %copy-done.2, bf16[96,128,128]{2,1,0:T(8,128)(2,1)S(1)} %bitcast.7, bf16[256,256]{1,0:T(8,128)(2,1)S(1)} %copy-done.1, ...), custom_call_target="tpu_custom_call" | custom-call | flops 2000000000 | bytes 4000000 | tf_op jit(solution)/shard_map/pallas_call | solution.py:515
  129.1 0.7 broadcast_multiply_fusion
  129.8 0.6 copy.13
  130.4 0.6 copy.14
  (15 shorter events, 0.1 us)
Async XLA Ops:
  7.4 1.9 %copy-start = (bf16[1,1,1,96,128,128]{5,4,3,2,1,0:T(8,128)(2,1)S(1)}, bf16[1,1,1,96,128,128]{5,4,3,2,1,0:T(8,128)(2,1)}, u32[]{:S(2)}) copy-start(bf16[1,1,1,96,128,128]{5,4,3,2,1,0:T(8,128)(2,1)} %param.8) | copy-start | bytes 9437188
  9.2 0.9 copy-start.1
  10.2 0.8 copy-start.2
  11.0 0.8 copy-start.3

commit v2 on v0

v2 whole, which is shorter than its diff:
```python
import jax
import jax.numpy as jnp
from jax import lax
from jax.experimental import pallas as pl
from jax.experimental.pallas import tpu as pltpu
from jax.sharding import PartitionSpec as P

MESH = pl.DeviceIdType.MESH
BF, F32 = jnp.bfloat16, jnp.float32

NX, NY, NZ = 4, 4, 16
TILE, F, SLOTS = 128, 256, 96
NROWS, NCOLS = NZ, NX * NY * 2
FPOS, BPOS = SLOTS + NROWS, SLOTS + NCOLS
FPAIRS, BPAIRS = FPOS // 2, BPOS // 2
Q = 2
REL = (2, 1, 3, 0)

F_IDX, F_OTH, F_KEEP, F_LAST, B_IDX, B_OTH, B_KEEP, B_LAST = range(8)


def schedule(keys, others, count, zero, none):
    full = (128, 128)
    lane, sub = lax.broadcasted_iota(jnp.int32, full, 1), lax.broadcasted_iota(jnp.int32, full, 0)

    def down(ref):
        return jnp.transpose(jnp.broadcast_to(ref, full))

    key = jnp.broadcast_to(keys, full)
    key_down = jnp.transpose(key)
    live = lane < count
    same = (key == key_down) & (sub < lane) & (sub < count)
    rank = jnp.sum(jnp.where(same, 1, 0), axis=0, keepdims=True)
    hot = (key == sub) & live
    number = jnp.sum(jnp.where(hot, 1, 0), axis=1, keepdims=True)
    padded = jnp.broadcast_to(lax.shift_left(lax.shift_right_logical(number + 1, 1), 1), full)
    place = rank + jnp.sum(jnp.where(sub < key, padded, 0), axis=0, keepdims=True)
    place = jnp.where(live, jnp.broadcast_to(place, full), 1000)
    at = jnp.transpose(place) == lane
    slot = jnp.sum(jnp.where(at, sub, 0), axis=0, keepdims=True)
    other = jnp.sum(jnp.where(at, down(others) - zero, 0), axis=0, keepdims=True) + zero
    keep = 1 - jnp.sum(jnp.where(at & (down(rank) == 0), 1, 0), axis=0, keepdims=True)
    last = jnp.max(jnp.where(hot, lax.shift_right_logical(place, 1), -1), axis=1, keepdims=True)
    last = down_first(jnp.where(number > 0, last, none), full)
    return [slot, other, keep, last]


def down_first(column, full):
    return jnp.transpose(jnp.broadcast_to(column, full))[:1]


def wait(ref, sem):
    pltpu.make_async_copy(ref, ref, sem).wait()


def kernel(
    counts, rows_i, cols_i, feats, tiles, weight, cot, hidden_o, gf_o, gw_o,
    rows_v, cols_v, pad, table_v, table, av, xg, fout, acc, wv, cv, zs, zr, gt, bout, sib_s, sib_r,
    ps, pr, qs, qr, vv, gft, gfv, hv,
    w1s, w1r, w2s, w2r, w3s, w3r, w4, w5, w6, w7, w8, lw, gwv,
    loc, ag_send, ag_recv, zs_send, zs_recv, zg_send, zg_recv,
    sb_send, sb_recv, rp_send, rp_recv, w_send, w_recv, out_sem,
):
    row, z, depth = lax.axis_index("row"), lax.axis_index("col"), lax.axis_index("depth")
    y, x, core = row // 2, (row % 2) * 2 + depth // 2, depth % 2

    def dev(dx=0, dy=0, dz=0, flip=0, zz=None):
        nx, ny = (x + dx) % NX, (y + dy) % NY
        nz = (z + dz + NZ) % NZ if zz is None else zz
        nc = (core + flip) % 2
        return {"row": ny * 2 + nx // 2, "col": nz, "depth": (nx % 2) * 2 + nc}

    def send(src, dst, ssem, rsem, to):
        pltpu.make_async_remote_copy(
            src_ref=src, dst_ref=dst, send_sem=ssem, recv_sem=rsem, device_id=to, device_id_type=MESH
        ).start()

    zi, zq = z % 4, z // 4
    partners = [dev(flip=1), dev(dz=1), dev(dz=-1), dev(dz=4), dev(dz=-4)]
    for k in (1, 2, 3):
        partners += [dev(dx=k), dev(dy=k), dev(zz=zq * 4 + (zi + k) % 4)]
    barrier = pltpu.get_barrier_semaphore()
    for to in partners:
        pl.semaphore_signal(barrier, inc=1, device_id=to, device_id_type=MESH)

    mine = 8 * y + 2 * x + core
    local = []
    for k, (src, dst) in enumerate(
        [(rows_i, rows_v), (cols_i, cols_v), (feats, xg.at[mine]), (tiles.at[0, 0, 0], av), (weight, wv), (cot, cv)]
    ):
        local.append(pltpu.make_async_copy(src, dst, loc.at[k]))
        local[k].start()
    pl.semaphore_wait(barrier, len(partners))

    def to_ab(h, da, db):
        return dev(dx=da, dy=db) if h == 0 else dev(dx=db, dy=da)

    def piece(h, da, db, flip=0):
        dx, dy = (da, db) if h == 0 else (db, da)
        return 8 * ((y + dy) % NY) + 2 * ((x + dx) % NX) + (core + flip) % 2

    def xpart(h, da, db, flip=0):
        return xg.at[piece(h, da, db, flip), pl.ds(64 * h, 64)]

    def forward(h, da, db, to, k, own):
        src = feats.at[pl.ds(64 * h, 64)] if own else xpart(h, da, db)
        send(src, xpart(h, da, db), ag_send, ag_recv.at[h, k], to)

    def to_a(h, k):
        forward(h, 0, 0, to_ab(h, k, 0), k - 1, True)

    def to_b(h, e, k, own=False):
        forward(h, e, 0, to_ab(h, 0, k), 3 + 3 * e + k - 1, own)

    def to_sib(h, da, db, own=False):
        forward(h, da, db, dev(flip=1), 15 + 4 * da + db, own)

    for k in (2, 1, 3):
        for h in (0, 1):
            to_a(h, k)
    for k in (2, 1, 3):
        for h in (0, 1):
            to_b(h, 0, k, True)
    for h in (0, 1):
        to_sib(h, 0, 0, True)

    xg[NCOLS] = jnp.zeros((TILE, F), BF)
    gt[NZ] = jnp.zeros((F, TILE), BF)
    fout[FPAIRS] = jnp.zeros((TILE, F), BF)
    bout[BPAIRS] = jnp.zeros((F, TILE), BF)
    acc[...] = jnp.zeros_like(acc)
    pad[...] = jnp.zeros_like(pad)
    local[0].wait()
    local[1].wait()
    pad[0:1, 0:SLOTS] = rows_v[0, 0]
    pad[1:2, 0:SLOTS] = cols_v[0, 0]
    live_count = counts[0, 0, 0]
    by_row = schedule(pad[0:1], pad[1:2], live_count, NCOLS, FPAIRS)
    by_col = schedule(pad[1:2], pad[0:1], live_count, NZ, BPAIRS)
    for k, line in enumerate(by_row + by_col):
        table_v[k : k + 1, :] = line
    table_copy = pltpu.make_async_copy(table_v, table, loc.at[6])
    table_copy.start()

    for k in (1, 3, 2):
        for h in (0, 1):
            wait(xpart(h, 4 - k, 0), ag_recv.at[h, k - 1])
            for kb in (2, 1, 3):
                to_b(h, 4 - k, kb)
            to_sib(h, 4 - k, 0)
    for e in (0, 3, 1, 2):
        for k in (1, 3, 2):
            for h in (0, 1):
                wait(xpart(h, e, 4 - k), ag_recv.at[h, 3 + 3 * e + k - 1])
                to_sib(h, e, 4 - k)
    for h in (0, 1):
        for da in range(4):
            for db in range(4):
                wait(xpart(h, da, db, 1), ag_recv.at[h, 15 + 4 * da + db])
    for copy in local[2:]:
        copy.wait()
    table_copy.wait()

    def forward_pair(q, carry):
        a = jnp.concatenate([av[table[F_IDX, 2 * q]], av[table[F_IDX, 2 * q + 1]]], axis=1)
        b = jnp.concatenate([xg[table[F_OTH, 2 * q]], xg[table[F_OTH, 2 * q + 1]]], axis=0)
        keep = table[F_KEEP, 2 * q].astype(F32)
        total = acc[...] * keep + jnp.dot(a, b, preferred_element_type=F32)
        acc[...] = total
        fout[q] = total.astype(BF)
        return carry

    lax.fori_loop(0, FPAIRS, forward_pair, 0, unroll=4)

    ROWS = TILE // Q

    def farthest(d, q):
        return 8 if (d == 0) == (q % 2 == 0) else 7

    def zat(d, dist):
        return (z + dist) % NZ if d == 0 else (z - dist + NZ) % NZ

    def zto(d, step=1):
        return dev(dz=step if d == 0 else -step)

    def sum_hop(dist):
        for q in range(Q):
            part = pl.ds(q * ROWS, ROWS)
            for d in (0, 1):
                far = farthest(d, q)
                if dist > far:
                    continue
                term = fout[table[F_LAST, zat(d, dist)], part, :]
                if dist not in (far, 3):
                    wait(zr.at[d, dist, part], zs_recv.at[d, dist, q])
                    term = (term.astype(F32) + zr[d, dist, part, :].astype(F32)).astype(BF)
                zs[d, dist - 1, part, :] = term
                send(
                    zs.at[d, dist - 1, part], zr.at[d, 0 if dist == 4 else (8 if dist == 1 else dist - 1), part], zs_send,
                    zs_recv.at[d, 8 if dist == 4 else dist - 1, q], zto(d, 4 if dist == 4 else 1),
                )

    for dist in (8, 7, 3, 6, 2, 5, 1, 4):
        sum_hop(dist)
    totals = []
    for q in range(Q):
        part = pl.ds(q * ROWS, ROWS)
        total = fout[table[F_LAST, z], part, :].astype(F32)
        for d in (0, 1):
            for slot, sem in ((8, 0), (0, 8)):
                wait(zr.at[d, slot, part], zs_recv.at[d, sem, q])
                total = total + zr[d, slot, part, :].astype(F32)
        totals.append(total.astype(BF))
    agg = jnp.concatenate(totals, axis=0)

    w = wv[...]
    pre = jnp.dot(agg, w, preferred_element_type=F32)
    sig = jax.nn.sigmoid(pre)
    grad_pre = (cv[...].astype(F32) * sig * (1.0 + pre * (1.0 - sig))).astype(BF)
    gt[z] = lax.dot_general(w, grad_pre, (((1,), (1,)), ((), ())), preferred_element_type=F32).astype(BF)

    FR = F // Q

    def gather_from(dist):
        for q in range(Q):
            part = pl.ds(q * FR, FR)
            for d in (0, 1):
                far = farthest(d, q)
                if dist > far:
                    continue
                ref = gt.at[zat(1 - d, dist), part]
                if dist > 0:
                    wait(ref, zg_recv.at[d, dist, q])
                if dist == 0:
                    send(ref, ref, zg_send, zg_recv.at[d, 4, q], zto(d, 4))
                if dist != 3 and dist < far:
                    send(ref, ref, zg_send, zg_recv.at[d, dist + 1, q], zto(d))

    gather_from(0)
    hv[...] = (pre * sig).astype(BF)
    hidden_copy = pltpu.make_async_copy(hv, hidden_o, out_sem.at[0])
    hidden_copy.start()
    lw[...] = lax.dot_general(agg, grad_pre, (((0,), (0,)), ((), ())), preferred_element_type=F32)
    for k in range(4):
        w1s[k] = lw[pl.ds(64 * k, 64), :].astype(BF)

    def w_stage1():
        for k in (1, 2, 3):
            send(w1s.at[(y + k) % NY], w1r.at[k - 1], w_send.at[0], w_recv.at[0], dev(dy=k))

    def w_stage2():
        wait(w1r, w_recv.at[0])
        total = lw[pl.ds(pl.multiple_of(64 * y, 64), 64), :]
        for k in range(3):
            total = total + w1r[k].astype(F32)
        for k in range(4):
            w2s[k] = total[16 * k : 16 * k + 16, :].astype(BF)
        for k in (1, 2, 3):
            send(w2s.at[(x + k) % NX], w2r.at[k - 1], w_send.at[1], w_recv.at[1], dev(dx=k))

    def w_stage3():
        wait(w2r, w_recv.at[1])
        total = w2s[x].astype(F32)
        for k in range(3):
            total = total + w2r[k].astype(F32)
        w3s[0] = total[:, :128].astype(BF)
        w3s[1] = total[:, 128:].astype(BF)
        send(w3s.at[1 - core], w3r, w_send.at[2], w_recv.at[2], dev(flip=1))

    def w_stage4():
        wait(w3r, w_recv.at[2])
        w4[zi] = (w3s[core].astype(F32) + w3r[...].astype(F32)).astype(BF)
        for k in (1, 2, 3):
            send(w4.at[zi], w4.at[zi], w_send.at[3], w_recv.at[3], dev(zz=zq * 4 + (zi + k) % 4))

    def sum4(ref):
        total = ref[0].astype(F32)
        for k in (1, 2, 3):
            total = total + ref[k].astype(F32)
        return total.astype(BF)

    def w_stage5():
        wait(w4.at[pl.ds(0, 3)], w_recv.at[3])
        w5[zq] = sum4(w4)
        for d in (0, 1):
            send(w5.at[zq], w5.at[zq], w_send.at[4], w_recv.at[4 + d], zto(d, 4))

    def w_stage6():
        for d in (0, 1):
            wait(w5.at[(zq + 3 + 2 * d) % 4], w_recv.at[4 + d])
        send(w5.at[(zq + 3) % 4], w5.at[(zq + 3) % 4], w_send.at[5], w_recv.at[6], dev(dz=4))

    def w_stage7():
        wait(w5.at[(zq + 2) % 4], w_recv.at[6])
        w6[core] = sum4(w5)
        send(w6.at[core], w6.at[core], w_send.at[6], w_recv.at[7], dev(flip=1))

    def w_stage8():
        wait(w6.at[1 - core], w_recv.at[7])
        w7[x] = w6[...]
        for k in (1, 2, 3):
            send(w7.at[x], w7.at[x], w_send.at[7], w_recv.at[8], dev(dx=k))

    def w_stage9():
        wait(w7.at[pl.ds(0, 3)], w_recv.at[8])
        w8[y] = w7[...]
        for k in (1, 2, 3):
            send(w8.at[y], w8.at[y], w_send.at[8], w_recv.at[9], dev(dy=k))

    def w_stage10():
        wait(w8.at[pl.ds(0, 3)], w_recv.at[9])
        scale = (TILE * NX * NY * NZ * 2) ** -0.5
        for i in range(4):
            for j in range(4):
                for k in range(2):
                    gwv[pl.ds(64 * i + 16 * j, 16), pl.ds(128 * k, 128)] = w8[i, j, k].astype(F32) * scale
        gw_copy = pltpu.make_async_copy(gwv, gw_o, out_sem.at[1])
        gw_copy.start()
        return gw_copy

    w_stage1()
    gather_from(1)
    gather_from(2)
    w_stage2()
    gather_from(4)
    gather_from(5)
    w_stage3()
    gather_from(6)
    w_stage4()
    gather_from(7)
    gather_from(3)
    gather_from(8)
    w_stage5()

    def products(h):
        half = pl.ds(128 * h, 128)

        def backward_pair(q, carry):
            a = jnp.concatenate([gt[table[B_OTH, 2 * q], half, :], gt[table[B_OTH, 2 * q + 1], half, :]], axis=1)
            b = jnp.concatenate([av[table[B_IDX, 2 * q]], av[table[B_IDX, 2 * q + 1]]], axis=0)
            keep = table[B_KEEP, 2 * q].astype(F32)
            total = gfv[half, :] * keep + jnp.dot(a, b, preferred_element_type=F32)
            gfv[half, :] = total
            bout[q, half, :] = total.astype(BF)
            return carry

        gfv[half, :] = jnp.zeros((128, TILE), F32)
        lax.fori_loop(0, BPAIRS, backward_pair, 0, unroll=4)

    def term(h, g, e, flip=0):
        dx, dy = (e, g) if h == 0 else (g, e)
        c = 8 * ((y + dy) % NY) + 2 * ((x + dx) % NX) + (core + flip) % 2
        return bout[table[B_LAST, c], pl.ds(128 * h, 128), :]

    def to_h(h, da, db):
        return dev(dx=db, dy=da) if h == 0 else dev(dx=da, dy=db)

    def to_sibling(h):
        for g in range(4):
            for e in range(4):
                sib_s[h, g, e] = term(h, REL[g], REL[e], 1)
            send(sib_s.at[h, g], sib_r.at[h, g], sb_send, sb_recv.at[h, g], dev(flip=1))

    def both(h, g, e):
        return term(h, REL[g], REL[e]).astype(F32) + sib_r[h, g, e].astype(F32)

    def first_axis(h):
        for g in range(3):
            wait(sib_r.at[h, g], sb_recv.at[h, g])
            for e in range(4):
                ps[h, g, e] = both(h, g, e).astype(BF)
            send(ps.at[h, g], pr.at[h, g], rp_send.at[0], rp_recv.at[h, g], to_h(h, REL[g], 0))

    def second_axis(h):
        wait(sib_r.at[h, 3], sb_recv.at[h, 3])
        for g in range(3):
            wait(pr.at[h, g], rp_recv.at[h, g])
        for e in range(4):
            total = both(h, 3, e)
            for g in range(3):
                total = total + pr[h, g, e].astype(F32)
            if e < 3:
                qs[h, e] = total.astype(BF)
                send(qs.at[h, e], qr.at[h, e], rp_send.at[1], rp_recv.at[h, 3 + e], to_h(h, 0, REL[e]))
            else:
                vv[h] = total

    products(0)
    to_sibling(0)
    w_stage6()
    products(1)
    to_sibling(1)
    first_axis(0)
    first_axis(1)
    w_stage7()
    second_axis(0)
    w_stage8()
    second_axis(1)
    w_stage9()
    for h in (0, 1):
        total = vv[h]
        for e in range(3):
            wait(qr.at[h, e], rp_recv.at[h, 3 + e])
            total = total + qr[h, e].astype(F32)
        gft[pl.ds(128 * h, 128), :] = total
    hv2 = xg.at[NCOLS]
    hv2[...] = jnp.transpose(gft[...]).astype(BF)
    gf_copy = pltpu.make_async_copy(hv2, gf_o, out_sem.at[2])
    gf_copy.start()
    gw_copy = w_stage10()

    hidden_copy.wait()
    gw_copy.wait()
    gf_copy.wait()
    wait(xg.at[pl.ds(0, NCOLS - 1)], ag_send)
    wait(xg.at[pl.ds(0, NZ - 1)], zs_send)
    wait(xg.at[pl.ds(0, NZ - 1)], zg_send)
    wait(sib_s, sb_send)
    wait(ps, rp_send.at[0])
    wait(qs, rp_send.at[1])
    wait(w1r, w_send.at[0])
    wait(w2r, w_send.at[1])
    wait(w3r, w_send.at[2])
    wait(w4.at[pl.ds(0, 3)], w_send.at[3])
    wait(w5.at[pl.ds(0, 2)], w_send.at[4])
    wait(w5.at[0], w_send.at[5])
    wait(w6.at[0], w_send.at[6])
    wait(w7.at[pl.ds(0, 3)], w_send.at[7])
    wait(w8.at[pl.ds(0, 3)], w_send.at[8])


def per_device(feats, tile_values, tile_rows, tile_cols, tile_count, weight, cotangent):
    vm, dma = pltpu.VMEM, pltpu.SemaphoreType.DMA
    scratch = [
        vm((1, 1, 1, SLOTS), jnp.int32),
        vm((1, 1, 1, SLOTS), jnp.int32),
        vm((8, 128), jnp.int32),
        vm((8, 128), jnp.int32),
        pltpu.SMEM((8, 128), jnp.int32),
        vm((SLOTS, TILE, TILE), BF),
        vm((NCOLS + 1, TILE, F), BF),
        vm((FPAIRS + 1, TILE, F), BF),
        vm((TILE, F), F32),
        vm((F, F), BF),
        vm((TILE, F), BF),
        vm((2, 8, TILE, F), BF),
        vm((2, 9, TILE, F), BF),
        vm((NZ + 1, F, TILE), BF),
        vm((BPAIRS + 1, F, TILE), BF),
        vm((2, 4, 4, 128, TILE), BF),
        vm((2, 4, 4, 128, TILE), BF),
        vm((2, 3, 4, 128, TILE), BF),
        vm((2, 3, 4, 128, TILE), BF),
        vm((2, 3, 128, TILE), BF),
        vm((2, 3, 128, TILE), BF),
        vm((2, 128, TILE), F32),
        vm((F, TILE), F32),
        vm((F, TILE), F32),
        vm((TILE, F), BF),
        vm((4, 64, F), BF),
        vm((3, 64, F), BF),
        vm((4, 16, F), BF),
        vm((3, 16, F), BF),
        vm((2, 16, 128), BF),
        vm((16, 128), BF),
        vm((4, 16, 128), BF),
        vm((4, 16, 128), BF),
        vm((2, 16, 128), BF),
        vm((4, 2, 16, 128), BF),
        vm((4, 4, 2, 16, 128), BF),
        vm((F, F), F32),
        vm((F, F), F32),
        dma((7,)),
        dma,
        dma((2, 31)),
        dma,
        dma((2, 9, Q)),
        dma,
        dma((2, 9, Q)),
        dma,
        dma((2, 4)),
        dma((2,)),
        dma((2, 6)),
        dma((9,)),
        dma((10,)),
        dma((3,)),
    ]
    any_spec = pl.BlockSpec(memory_space=pltpu.HBM)
    hidden, grad_feats, grad_weight = pl.pallas_call(
        kernel,
        out_shape=(
            jax.ShapeDtypeStruct((TILE, F), BF),
            jax.ShapeDtypeStruct((TILE, F), BF),
            jax.ShapeDtypeStruct((F, F), F32),
        ),
        in_specs=[pl.BlockSpec(memory_space=pltpu.SMEM)] + [any_spec] * 6,
        out_specs=(any_spec,) * 3,
        scratch_shapes=scratch,
        compiler_params=pltpu.CompilerParams(
            collective_id=0, has_side_effects=True, vmem_limit_bytes=60 * 1024 * 1024
        ),
        cost_estimate=pl.CostEstimate(flops=2_000_000_000, bytes_accessed=4_000_000, transcendentals=32768),
    )(tile_count, tile_rows, tile_cols, feats, tile_values, weight, cotangent)
    return hidden, grad_feats, grad_weight


def solution(mesh):
    return jax.shard_map(
        per_device,
        mesh=mesh,
        in_specs=(
            P(("row", "col", "depth"), None),
            P("row", "col", "depth", None, None, None),
            P("row", "col", "depth", None),
            P("row", "col", "depth", None),
            P("row", "col", "depth"),
            P(),
            P(("row", "col", "depth"), None),
        ),
        out_specs=(P(("row", "col", "depth"), None), P(("row", "col", "depth"), None), P()),
        check_vma=False,
    )
```

time: 826 us -> 106 us (0.13)
  waiting for transfers between devices: 723 us -> 0 us
  Pallas kernels: 0 us -> 99.8 us
  matrix products: 40.2 us -> 0 us
  local copies, waits for them, and re-layouts: 44 us -> 4.61 us
  between operations: 14.6 us -> 1.29 us
    psum x1 -> x0, waiting for transfers between devices: 429 us -> none  [per_device(): lax.psum(local_weight, ('row', 'col', 'depth')) * nodes_all ** (-0.5)]
    reduce_scatter x2 -> x0, waiting for transfers between devices: 160 us -> none  [the longest x1 101 us: per_device(): lax.psum_scatter(vertical_partial_terms.astype(jnp.bfloat16), ('row', 'de...]
    all_gather x2 -> x0, waiting for transfers between devices: 134 us -> none  [the longest x1 67.5 us: per_device(): lax.all_gather(grad_agg, 'col', axis=0, tiled=True)]
    pallas_call x0 -> x1, Pallas kernels: none -> 99.8 us  [per_device(): pl.pallas_call(kernel, out_shape=(jax.ShapeDtypeStruct((TILE, F), BF), ja...]
    dot_general x7 -> x0, matrix products: 40.2 us -> none  [the longest x1 9.15 us: per_device(): jnp.einsum('kab,kbf->kaf', tile_vals, picked, preferred_element_type=jnp....]
    dot_general x2 -> x0, local copies, waits for them, and re-layouts: 25.4 us -> none  [the longest x1 12.7 us: per_device(): jnp.einsum('kab,kbf->kaf', tile_vals, picked, preferred_element_type=jnp....]
    gather x2 -> x0, local copies, waits for them, and re-layouts: 14.7 us -> none  [the longest x1 7.53 us: per_device(): picked = gathered[tile_col]]
  transfers between devices with their start and end apart: 5 -> 0, of which waited for: 5 -> 0; matrix products, arithmetic and copies ran while one was open for 5% -> 0% of each run, Pallas kernels for 0% -> 0%
where the time goes in v2:
time: 106 us
  Pallas kernels  99.8 us (94%)
  local copies, waits for them, and re-layouts  4.61 us (4%)
  between operations  1.29 us (1%)
    pallas_call x1, Pallas kernels, per_device(): pl.pallas_call(kernel, out_shape=(jax.ShapeDtypeStruct((TILE, F), BF), ja...  99.8 us
    unnamed x3, local copies, waits for them, and re-layouts  4.61 us

profile of v2, /device:TPU:1, one launch (start us, length us, event | category | flops | bytes accessed | tf_op | source)
XLA Modules:
  0.0 105.7 jit_solution(16387604036558069031)
XLA Ops:
  1.3 99.8 %shard_map.94 = (bf16[128,256]{1,0:T(8,128)(2,1)}, bf16[128,256]{1,0:T(8,128)(2,1)}, f32[256,256]{1,0:T(8,128)}) custom-call(s32[1,1,1]{2,1,0:T(1,128)S(6)} %copy.13.counts, s32[1,1,1,96]{3,2,1,0:T(1,128)} %rows_i.1, s32[1,1,1,96]{3,2,1,0:T(1,128)} %cols_i.1, bf16[128,256]{1,0:T(8,128)(2,1)} %feats.1, bf16[1,1,1,96,128,128]{5,4,3,2,1,0:T(8,128)(2,1)} %tiles.1, ...), custom_call_target="tpu_custom_call" | custom-call | flops 2000000000 | bytes 4000000 | tf_op jit(solution)/shard_map/pallas_call | solution.py:489
  101.1 1.5 %copy.14 = bf16[128,256]{1,0:T(8,128)(2,1)} copy(bf16[128,256]{1,0:T(8,128)(2,1)} %get-tuple-element.6) | data formatting | bytes 131072
  102.5 1.5 %copy.15 = bf16[128,256]{1,0:T(8,128)(2,1)} copy(bf16[128,256]{1,0:T(8,128)(2,1)} %get-tuple-element.7) | data formatting | bytes 131072
  104.0 1.7 %copy.16 = f32[256,256]{1,0:T(8,128)} copy(f32[256,256]{1,0:T(8,128)} %get-tuple-element.8) | data formatting | bytes 524288

commit v3 on v2

--- a/solution.py
+++ b/solution.py
@@ -55,7 +55,7 @@
 
 def kernel(
     counts, rows_i, cols_i, feats, tiles, weight, cot, hidden_o, gf_o, gw_o,
-    rows_v, cols_v, pad, table_v, table, av, xg, fout, acc, wv, cv, zs, zr, gt, bout, sib_s, sib_r,
+    rows_v, cols_v, pad, table_v, table, av, xg, fout, acc, wv, cv, zs, zr, gt0, gt1, bout, sib_s, sib_r,
     ps, pr, qs, qr, vv, gft, gfv, hv,
     w1s, w1r, w2s, w2r, w3s, w3r, w4, w5, w6, w7, w8, lw, gwv,
     loc, ag_send, ag_recv, zs_send, zs_recv, zg_send, zg_recv,
@@ -76,7 +76,7 @@
         ).start()
 
     zi, zq = z % 4, z // 4
-    partners = [dev(flip=1), dev(dz=1), dev(dz=-1), dev(dz=4), dev(dz=-4)]
+    partners = [dev(flip=1)] + [dev(dz=step) for step in (1, -1, 2, -2, 4, -4)]
     for k in (1, 2, 3):
         partners += [dev(dx=k), dev(dy=k), dev(zz=zq * 4 + (zi + k) % 4)]
     barrier = pltpu.get_barrier_semaphore()
@@ -125,7 +125,8 @@
         to_sib(h, 0, 0, True)
 
     xg[NCOLS] = jnp.zeros((TILE, F), BF)
-    gt[NZ] = jnp.zeros((F, TILE), BF)
+    for part in (gt0, gt1):
+        part[NZ] = jnp.zeros((F // 2, TILE), BF)
     fout[FPAIRS] = jnp.zeros((TILE, F), BF)
     bout[BPAIRS] = jnp.zeros((F, TILE), BF)
     acc[...] = jnp.zeros_like(acc)
@@ -134,7 +135,7 @@
     local[1].wait()
     pad[0:1, 0:SLOTS] = rows_v[0, 0]
     pad[1:2, 0:SLOTS] = cols_v[0, 0]
-    live_count = counts[0, 0, 0]
+    live_count = jnp.broadcast_to(counts[0], (128, 128))
     by_row = schedule(pad[0:1], pad[1:2], live_count, NCOLS, FPAIRS)
     by_col = schedule(pad[1:2], pad[0:1], live_count, NZ, BPAIRS)
     for k, line in enumerate(by_row + by_col):
@@ -184,6 +185,7 @@
         return dev(dz=step if d == 0 else -step)
 
     def sum_hop(dist):
+        step = 2 - dist % 2
         for q in range(Q):
             part = pl.ds(q * ROWS, ROWS)
             for d in (0, 1):
@@ -191,24 +193,27 @@
                 if dist > far:
                     continue
                 term = fout[table[F_LAST, zat(d, dist)], part, :]
-                if dist not in (far, 3):
-                    wait(zr.at[d, dist, part], zs_recv.at[d, dist, q])
-                    term = (term.astype(F32) + zr[d, dist, part, :].astype(F32)).astype(BF)
+                if step == 2 and dist < 8:
+                    term = term.astype(F32)
+                    for other in (dist + 1, dist + 2):
+                        if other <= far:
+                            wait(zr.at[d, other - 1, part], zs_recv.at[d, other - 1, q])
+                            term = term + zr[d, other - 1, part, :].astype(F32)
+                    term = term.astype(BF)
                 zs[d, dist - 1, part, :] = term
                 send(
-                    zs.at[d, dist - 1, part], zr.at[d, 0 if dist == 4 else (8 if dist == 1 else dist - 1), part], zs_send,
-                    zs_recv.at[d, 8 if dist == 4 else dist - 1, q], zto(d, 4 if dist == 4 else 1),
+                    zs.at[d, dist - 1, part], zr.at[d, dist - 1, part], zs_send, zs_recv.at[d, dist - 1, q], zto(d, step)
                 )
 
-    for dist in (8, 7, 3, 6, 2, 5, 1, 4):
+    for dist in (8, 7, 5, 6, 3, 4, 1, 2):
         sum_hop(dist)
     totals = []
     for q in range(Q):
         part = pl.ds(q * ROWS, ROWS)
         total = fout[table[F_LAST, z], part, :].astype(F32)
         for d in (0, 1):
-            for slot, sem in ((8, 0), (0, 8)):
-                wait(zr.at[d, slot, part], zs_recv.at[d, sem, q])
+            for slot in (0, 1):
+                wait(zr.at[d, slot, part], zs_recv.at[d, slot, q])
                 total = total + zr[d, slot, part, :].astype(F32)
         totals.append(total.astype(BF))
     agg = jnp.concatenate(totals, axis=0)
@@ -217,34 +222,41 @@
     pre = jnp.dot(agg, w, preferred_element_type=F32)
     sig = jax.nn.sigmoid(pre)
     grad_pre = (cv[...].astype(F32) * sig * (1.0 + pre * (1.0 - sig))).astype(BF)
-    gt[z] = lax.dot_general(w, grad_pre, (((1,), (1,)), ((), ())), preferred_element_type=F32).astype(BF)
+    grad_agg = lax.dot_general(w, grad_pre, (((1,), (1,)), ((), ())), preferred_element_type=F32).astype(BF)
+    gts = (gt0, gt1)
+    for h in (0, 1):
+        gts[h][z] = grad_agg[128 * h : 128 * h + 128]
 
     FR = F // Q
 
-    def gather_from(dist):
-        for q in range(Q):
-            part = pl.ds(q * FR, FR)
-            for d in (0, 1):
-                far = farthest(d, q)
-                if dist > far:
-                    continue
-                ref = gt.at[zat(1 - d, dist), part]
-                if dist > 0:
-                    wait(ref, zg_recv.at[d, dist, q])
-                if dist == 0:
-                    send(ref, ref, zg_send, zg_recv.at[d, 4, q], zto(d, 4))
-                if dist != 3 and dist < far:
-                    send(ref, ref, zg_send, zg_recv.at[d, dist + 1, q], zto(d))
-
-    gather_from(0)
+    def halves(h):
+        return [(pl.ds(k * FR, FR), h * Q // 2 + k, d) for k in range(Q // 2) for d in (0, 1)]
+
+    def gather_from(dist, h):
+        for part, q, d in halves(h):
+            ref = gts[h].at[zat(1 - d, dist), part]
+            if dist > 0:
+                wait(ref, zg_recv.at[d, dist - 1, q])
+            for step in (2, 1):
+                if dist + step <= farthest(d, q):
+                    send(ref, ref, zg_send, zg_recv.at[d, dist + step - 1, q], zto(d, step))
+
+    def gather_end(h):
+        for dist in (1, 3, 5, 7, 8):
+            for part, q, d in halves(h):
+                if dist <= farthest(d, q):
+                    wait(gts[h].at[zat(1 - d, dist), part], zg_recv.at[d, dist - 1, q])
+
+    gather_from(0, 0)
+    gather_from(0, 1)
     hv[...] = (pre * sig).astype(BF)
     hidden_copy = pltpu.make_async_copy(hv, hidden_o, out_sem.at[0])
     hidden_copy.start()
-    lw[...] = lax.dot_general(agg, grad_pre, (((0,), (0,)), ((), ())), preferred_element_type=F32)
-    for k in range(4):
-        w1s[k] = lw[pl.ds(64 * k, 64), :].astype(BF)
 
     def w_stage1():
+        lw[...] = lax.dot_general(agg, grad_pre, (((0,), (0,)), ((), ())), preferred_element_type=F32)
+        for k in range(4):
+            w1s[k] = lw[pl.ds(64 * k, 64), :].astype(BF)
         for k in (1, 2, 3):
             send(w1s.at[(y + k) % NY], w1r.at[k - 1], w_send.at[0], w_recv.at[0], dev(dy=k))
 
@@ -319,24 +331,23 @@
         return gw_copy
 
     w_stage1()
-    gather_from(1)
-    gather_from(2)
+    gather_from(2, 0)
+    gather_from(2, 1)
     w_stage2()
-    gather_from(4)
-    gather_from(5)
+    gather_from(4, 0)
+    gather_from(4, 1)
     w_stage3()
-    gather_from(6)
+    gather_from(6, 0)
+    gather_from(6, 1)
     w_stage4()
-    gather_from(7)
-    gather_from(3)
-    gather_from(8)
+    gather_end(0)
     w_stage5()
 
-    def products(h):
+    def products(h, first, end):
         half = pl.ds(128 * h, 128)
 
         def backward_pair(q, carry):
-            a = jnp.concatenate([gt[table[B_OTH, 2 * q], half, :], gt[table[B_OTH, 2 * q + 1], half, :]], axis=1)
+            a = jnp.concatenate([gts[h][table[B_OTH, 2 * q]], gts[h][table[B_OTH, 2 * q + 1]]], axis=1)
             b = jnp.concatenate([av[table[B_IDX, 2 * q]], av[table[B_IDX, 2 * q + 1]]], axis=0)
             keep = table[B_KEEP, 2 * q].astype(F32)
             total = gfv[half, :] * keep + jnp.dot(a, b, preferred_element_type=F32)
@@ -344,71 +355,81 @@
             bout[q, half, :] = total.astype(BF)
             return carry
 
-        gfv[half, :] = jnp.zeros((128, TILE), F32)
-        lax.fori_loop(0, BPAIRS, backward_pair, 0, unroll=4)
-
-    def term(h, g, e, flip=0):
-        dx, dy = (e, g) if h == 0 else (g, e)
+        if first == 0:
+            gfv[half, :] = jnp.zeros((128, TILE), F32)
+        lax.fori_loop(first, end, backward_pair, 0, unroll=4)
+
+    def term(u, g, e, flip=0):
+        dx, dy = (e, g) if u % 2 == 0 else (g, e)
         c = 8 * ((y + dy) % NY) + 2 * ((x + dx) % NX) + (core + flip) % 2
-        return bout[table[B_LAST, c], pl.ds(128 * h, 128), :]
-
-    def to_h(h, da, db):
-        return dev(dx=db, dy=da) if h == 0 else dev(dx=da, dy=db)
+        return bout[table[B_LAST, c], pl.ds(64 * u, 64), :]
+
+    def to_u(u, da, db):
+        return dev(dx=db, dy=da) if u % 2 == 0 else dev(dx=da, dy=db)
 
     def to_sibling(h):
         for g in range(4):
-            for e in range(4):
-                sib_s[h, g, e] = term(h, REL[g], REL[e], 1)
-            send(sib_s.at[h, g], sib_r.at[h, g], sb_send, sb_recv.at[h, g], dev(flip=1))
-
-    def both(h, g, e):
-        return term(h, REL[g], REL[e]).astype(F32) + sib_r[h, g, e].astype(F32)
+            for u in (2 * h, 2 * h + 1):
+                for e in range(4):
+                    sib_s[u, g, e] = term(u, REL[g], REL[e], 1)
+                send(sib_s.at[u, g], sib_r.at[u, g], sb_send, sb_recv.at[u, g], dev(flip=1))
+
+    def both(u, g, e):
+        return term(u, REL[g], REL[e]).astype(F32) + sib_r[u, g, e].astype(F32)
 
     def first_axis(h):
         for g in range(3):
-            wait(sib_r.at[h, g], sb_recv.at[h, g])
+            for u in (2 * h, 2 * h + 1):
+                wait(sib_r.at[u, g], sb_recv.at[u, g])
+                for e in range(4):
+                    ps[u, g, e] = both(u, g, e).astype(BF)
+                send(ps.at[u, g], pr.at[u, g], rp_send.at[0], rp_recv.at[u, g], to_u(u, REL[g], 0))
+
+    def second_axis(h):
+        for u in (2 * h, 2 * h + 1):
+            wait(sib_r.at[u, 3], sb_recv.at[u, 3])
+            for g in range(3):
+                wait(pr.at[u, g], rp_recv.at[u, g])
             for e in range(4):
-                ps[h, g, e] = both(h, g, e).astype(BF)
-            send(ps.at[h, g], pr.at[h, g], rp_send.at[0], rp_recv.at[h, g], to_h(h, REL[g], 0))
-
-    def second_axis(h):
-        wait(sib_r.at[h, 3], sb_recv.at[h, 3])
-        for g in range(3):
-            wait(pr.at[h, g], rp_recv.at[h, g])
-        for e in range(4):
-            total = both(h, 3, e)
-            for g in range(3):
-                total = total + pr[h, g, e].astype(F32)
-            if e < 3:
-                qs[h, e] = total.astype(BF)
-                send(qs.at[h, e], qr.at[h, e], rp_send.at[1], rp_recv.at[h, 3 + e], to_h(h, 0, REL[e]))
-            else:
-                vv[h] = total
-
-    products(0)
+                total = both(u, 3, e)
+                for g in range(3):
+                    total = total + pr[u, g, e].astype(F32)
+                if e < 3:
+                    qs[u, e] = total.astype(BF)
+                    send(qs.at[u, e], qr.at[u, e], rp_send.at[1], rp_recv.at[u, 3 + e], to_u(u, 0, REL[e]))
+                else:
+                    vv[u] = total
+
+    def last_sum(h):
+        for u in (2 * h, 2 * h + 1):
+            total = vv[u]
+            for e in range(3):
+                wait(qr.at[u, e], rp_recv.at[u, 3 + e])
+                total = total + qr[u, e].astype(F32)
+            gft[pl.ds(64 * u, 64), :] = total
+
+    MID = BPAIRS // 2
+    products(0, 0, BPAIRS)
     to_sibling(0)
     w_stage6()
-    products(1)
+    gather_end(1)
+    products(1, 0, MID)
+    first_axis(0)
+    products(1, MID, BPAIRS)
     to_sibling(1)
-    first_axis(0)
+    w_stage7()
     first_axis(1)
-    w_stage7()
+    w_stage8()
     second_axis(0)
-    w_stage8()
+    w_stage9()
     second_axis(1)
-    w_stage9()
-    for h in (0, 1):
-        total = vv[h]
-        for e in range(3):
-            wait(qr.at[h, e], rp_recv.at[h, 3 + e])
-            total = total + qr[h, e].astype(F32)
-        gft[pl.ds(128 * h, 128), :] = total
+    last_sum(0)
+    gw_copy = w_stage10()
+    last_sum(1)
     hv2 = xg.at[NCOLS]
     hv2[...] = jnp.transpose(gft[...]).astype(BF)
     gf_copy = pltpu.make_async_copy(hv2, gf_o, out_sem.at[2])
     gf_copy.start()
-    gw_copy = w_stage10()
-
     hidden_copy.wait()
     gw_copy.wait()
     gf_copy.wait()
@@ -429,6 +450,19 @@
     wait(w8.at[pl.ds(0, 3)], w_send.at[8])
 
 
+def hand_over(a, b, c, a_o, b_o, c_o, a_v, b_v, c_v, sem):
+    trips = [(a, a_v, a_o), (b, b_v, b_o), (c, c_v, c_o)]
+    into = [pltpu.make_async_copy(src, via, sem.at[0, k]) for k, (src, via, _) in enumerate(trips)]
+    out = [pltpu.make_async_copy(via, dst, sem.at[1, k]) for k, (_, via, dst) in enumerate(trips)]
+    for copy in into:
+        copy.start()
+    for first, second in zip(into, out):
+        first.wait()
+        second.start()
+    for copy in out:
+        copy.wait()
+
+
 def per_device(feats, tile_values, tile_rows, tile_cols, tile_count, weight, cotangent):
     vm, dma = pltpu.VMEM, pltpu.SemaphoreType.DMA
     scratch = [
@@ -444,16 +478,17 @@
         vm((F, F), BF),
         vm((TILE, F), BF),
         vm((2, 8, TILE, F), BF),
-        vm((2, 9, TILE, F), BF),
-        vm((NZ + 1, F, TILE), BF),
+        vm((2, 8, TILE, F), BF),
+        vm((NZ + 1, F // 2, TILE), BF),
+        vm((NZ + 1, F // 2, TILE), BF),
         vm((BPAIRS + 1, F, TILE), BF),
-        vm((2, 4, 4, 128, TILE), BF),
-        vm((2, 4, 4, 128, TILE), BF),
-        vm((2, 3, 4, 128, TILE), BF),
-        vm((2, 3, 4, 128, TILE), BF),
-        vm((2, 3, 128, TILE), BF),
-        vm((2, 3, 128, TILE), BF),
-        vm((2, 128, TILE), F32),
+        vm((4, 4, 4, 64, TILE), BF),
+        vm((4, 4, 4, 64, TILE), BF),
+        vm((4, 3, 4, 64, TILE), BF),
+        vm((4, 3, 4, 64, TILE), BF),
+        vm((4, 3, 64, TILE), BF),
+        vm((4, 3, 64, TILE), BF),
+        vm((4, 64, TILE), F32),
         vm((F, TILE), F32),
         vm((F, TILE), F32),
         vm((TILE, F), BF),
@@ -470,30 +505,30 @@
         vm((4, 4, 2, 16, 128), BF),
         vm((F, F), F32),
         vm((F, F), F32),
-        dma((7,)),
+        dma((8,)),
         dma,
         dma((2, 31)),
         dma,
-        dma((2, 9, Q)),
+        dma((2, 8, Q)),
         dma,
-        dma((2, 9, Q)),
+        dma((2, 8, Q)),
         dma,
-        dma((2, 4)),
+        dma((4, 4)),
         dma((2,)),
-        dma((2, 6)),
+        dma((4, 6)),
         dma((9,)),
         dma((10,)),
         dma((3,)),
     ]
     any_spec = pl.BlockSpec(memory_space=pltpu.HBM)
-    hidden, grad_feats, grad_weight = pl.pallas_call(
+    results = pl.pallas_call(
         kernel,
         out_shape=(
             jax.ShapeDtypeStruct((TILE, F), BF),
             jax.ShapeDtypeStruct((TILE, F), BF),
             jax.ShapeDtypeStruct((F, F), F32),
         ),
-        in_specs=[pl.BlockSpec(memory_space=pltpu.SMEM)] + [any_spec] * 6,
+        in_specs=[pl.BlockSpec(memory_space=pltpu.VMEM)] + [any_spec] * 6,
         out_specs=(any_spec,) * 3,
         scratch_shapes=scratch,
         compiler_params=pltpu.CompilerParams(
@@ -501,7 +536,15 @@
         ),
         cost_estimate=pl.CostEstimate(flops=2_000_000_000, bytes_accessed=4_000_000, transcendentals=32768),
     )(tile_count, tile_rows, tile_cols, feats, tile_values, weight, cotangent)
-    return hidden, grad_feats, grad_weight
+    return pl.pallas_call(
+        hand_over,
+        out_shape=[jax.ShapeDtypeStruct(a.shape, a.dtype) for a in results],
+        in_specs=[any_spec] * 3,
+        out_specs=[any_spec] * 3,
+        scratch_shapes=[vm(a.shape, a.dtype) for a in results] + [dma((2, 3))],
+        cost_estimate=pl.CostEstimate(flops=0, bytes_accessed=800_000, transcendentals=0),
+        compiler_params=pltpu.CompilerParams(vmem_limit_bytes=60 * 1024 * 1024),
+    )(*results)
 
 
 def solution(mesh):

time: 106 us -> 93.7 us (0.88)
  Pallas kernels: 99.8 us -> 92.3 us
  local copies, waits for them, and re-layouts: 4.61 us -> 0 us
    pallas_call x1, Pallas kernels: 99.8 us -> 90.5 us  [per_device(): pl.pallas_call(kernel, out_shape=(jax.ShapeDtypeStruct((TILE, F), BF), ja...]
    unnamed x3 -> x0, local copies, waits for them, and re-layouts: 4.61 us -> none
    pallas_call x0 -> x1, Pallas kernels: none -> 1.78 us  [per_device(): pl.pallas_call(hand_over, out_shape=[jax.ShapeDtypeStruct(a.shape, a.dtyp...]
where the time goes in v3:
time: 93.7 us; the launch traced here: 93.6 us
  Pallas kernels  92.3 us (99%)
  between operations  1.29 us (1%)
    pallas_call x1, Pallas kernels, per_device(): pl.pallas_call(kernel, out_shape=(jax.ShapeDtypeStruct((TILE, F), BF), ja...  90.5 us

profile of v3, /device:TPU:1, one launch (start us, length us, event | category | flops | bytes accessed | tf_op | source)
XLA Modules:
  0.0 93.6 jit_solution(10877072663602761115)
XLA Ops:
  1.3 90.5 %shard_map.94 = (bf16[128,256]{1,0:T(8,128)(2,1)}, bf16[128,256]{1,0:T(8,128)(2,1)}, f32[256,256]{1,0:T(8,128)}) custom-call(s32[1,1,1]{2,1,0:T(1,128)S(6)} %copy.10.counts, s32[1,1,1,96]{3,2,1,0:T(1,128)} %rows_i.1, s32[1,1,1,96]{3,2,1,0:T(1,128)} %cols_i.1, bf16[128,256]{1,0:T(8,128)(2,1)} %feats.1, bf16[1,1,1,96,128,128]{5,4,3,2,1,0:T(8,128)(2,1)} %tiles.1, ...), custom_call_target="tpu_custom_call" | custom-call | flops 2000000000 | bytes 4000000 | tf_op jit(solution)/shard_map/pallas_call | solution.py:524
  91.8 1.8 %shard_map.95 = (bf16[128,256]{1,0:T(8,128)(2,1)}, bf16[128,256]{1,0:T(8,128)(2,1)}, f32[256,256]{1,0:T(8,128)}) custom-call(bf16[128,256]{1,0:T(8,128)(2,1)} %get-tuple-element.6.a, bf16[128,256]{1,0:T(8,128)(2,1)} %get-tuple-element.7.b, f32[256,256]{1,0:T(8,128)} %get-tuple-element.8.c), custom_call_target="tpu_custom_call" | custom-call | bytes 800000 | tf_op jit(solution)/shard_map/pallas_call | solution.py:539

commit v4 on v3

--- a/solution.py
+++ b/solution.py
@@ -16,7 +16,7 @@
 Q = 2
 REL = (2, 1, 3, 0)
 
-F_IDX, F_OTH, F_KEEP, F_LAST, B_IDX, B_OTH, B_KEEP, B_LAST = range(8)
+F_IDX, F_OTH, F_KEEP, F_LAST, B_IDX, B_OTH, B_KEEP, B_LAST, F_OTH_B = range(9)
 
 
 def schedule(keys, others, count, zero, none):
@@ -55,9 +55,9 @@
 
 def kernel(
     counts, rows_i, cols_i, feats, tiles, weight, cot, hidden_o, gf_o, gw_o,
-    rows_v, cols_v, pad, table_v, table, av, xg, fout, acc, wv, cv, zs, zr, gt0, gt1, bout, sib_s, sib_r,
-    ps, pr, qs, qr, vv, gft, gfv, hv,
-    w1s, w1r, w2s, w2r, w3s, w3r, w4, w5, w6, w7, w8, lw, gwv,
+    rows_v, cols_v, pad, table_v, table, av, xa, xb, fout, wv, cv, zs, zr, gt0, gt1, bout, sib_s, sib_r,
+    ps, pr, qs, qr, vv, gft, gfv, hv, gf_v,
+    w1s, w1r, w2s, w2r, w3s, w3r, w4, w5, w7, w8, lw, gwv,
     loc, ag_send, ag_recv, zs_send, zs_recv, zg_send, zg_recv,
     sb_send, sb_recv, rp_send, rp_recv, w_send, w_recv, out_sem,
 ):
@@ -83,10 +83,12 @@
     for to in partners:
         pl.semaphore_signal(barrier, inc=1, device_id=to, device_id_type=MESH)
 
-    mine = 8 * y + 2 * x + core
+    xs = (xa, xb)
+    mine = (16 * core + 4 * y + x, 16 * core + 4 * x + y)
     local = []
     for k, (src, dst) in enumerate(
-        [(rows_i, rows_v), (cols_i, cols_v), (feats, xg.at[mine]), (tiles.at[0, 0, 0], av), (weight, wv), (cot, cv)]
+        [(rows_i, rows_v), (cols_i, cols_v), (tiles.at[0, 0, 0], av), (weight, wv), (cot, cv)]
+        + [(feats.at[pl.ds(64 * h, 64)], xs[h].at[mine[h]]) for h in (0, 1)]
     ):
         local.append(pltpu.make_async_copy(src, dst, loc.at[k]))
         local[k].start()
@@ -95,41 +97,33 @@
     def to_ab(h, da, db):
         return dev(dx=da, dy=db) if h == 0 else dev(dx=db, dy=da)
 
-    def piece(h, da, db, flip=0):
-        dx, dy = (da, db) if h == 0 else (db, da)
-        return 8 * ((y + dy) % NY) + 2 * ((x + dx) % NX) + (core + flip) % 2
-
-    def xpart(h, da, db, flip=0):
-        return xg.at[piece(h, da, db, flip), pl.ds(64 * h, 64)]
-
-    def forward(h, da, db, to, k, own):
-        src = feats.at[pl.ds(64 * h, 64)] if own else xpart(h, da, db)
-        send(src, xpart(h, da, db), ag_send, ag_recv.at[h, k], to)
-
-    def to_a(h, k):
-        forward(h, 0, 0, to_ab(h, k, 0), k - 1, True)
-
-    def to_b(h, e, k, own=False):
-        forward(h, e, 0, to_ab(h, 0, k), 3 + 3 * e + k - 1, own)
-
-    def to_sib(h, da, db, own=False):
-        forward(h, da, db, dev(flip=1), 15 + 4 * da + db, own)
+    along = ((x, y), (y, x))
+
+    def xpart(h, da, db):
+        return xs[h].at[16 * core + 4 * ((along[h][1] + db) % 4) + (along[h][0] + da) % 4]
+
+    def xline(h, db, flip=0):
+        return xs[h].at[pl.ds(16 * ((core + flip) % 2) + 4 * ((along[h][1] + db) % 4), 4)]
+
+    def own(h, da, db, k):
+        send(feats.at[pl.ds(64 * h, 64)], xpart(h, 0, 0), ag_send.at[h], ag_recv.at[h, k], to_ab(h, da, db))
+
+    def to_sib(h, db):
+        send(xline(h, db), xline(h, db), ag_send.at[h], ag_recv.at[h, 15 + db], dev(flip=1))
 
     for k in (2, 1, 3):
         for h in (0, 1):
-            to_a(h, k)
+            own(h, k, 0, k - 1)
     for k in (2, 1, 3):
         for h in (0, 1):
-            to_b(h, 0, k, True)
-    for h in (0, 1):
-        to_sib(h, 0, 0, True)
-
-    xg[NCOLS] = jnp.zeros((TILE, F), BF)
+            own(h, 0, k, 2 + k)
+
+    for part in xs:
+        part[NCOLS] = jnp.zeros((TILE // 2, F), BF)
     for part in (gt0, gt1):
         part[NZ] = jnp.zeros((F // 2, TILE), BF)
     fout[FPAIRS] = jnp.zeros((TILE, F), BF)
     bout[BPAIRS] = jnp.zeros((F, TILE), BF)
-    acc[...] = jnp.zeros_like(acc)
     pad[...] = jnp.zeros_like(pad)
     local[0].wait()
     local[1].wait()
@@ -138,40 +132,47 @@
     live_count = jnp.broadcast_to(counts[0], (128, 128))
     by_row = schedule(pad[0:1], pad[1:2], live_count, NCOLS, FPAIRS)
     by_col = schedule(pad[1:2], pad[0:1], live_count, NZ, BPAIRS)
-    for k, line in enumerate(by_row + by_col):
+    piece = by_row[1]
+    py, px, pc = lax.shift_right_logical(piece, 3), lax.shift_right_logical(piece, 1) & 3, piece & 1
+    by_row[1] = jnp.where(piece < NCOLS, 16 * pc + 4 * py + px, NCOLS)
+    by_x = jnp.where(piece < NCOLS, 16 * pc + 4 * px + py, NCOLS)
+    for k, line in enumerate(by_row + by_col + [by_x]):
         table_v[k : k + 1, :] = line
-    table_copy = pltpu.make_async_copy(table_v, table, loc.at[6])
+    table_copy = pltpu.make_async_copy(table_v, table, loc.at[7])
     table_copy.start()
 
+    local[5].wait()
+    local[6].wait()
     for k in (1, 3, 2):
         for h in (0, 1):
             wait(xpart(h, 4 - k, 0), ag_recv.at[h, k - 1])
+            src = xpart(h, 4 - k, 0)
             for kb in (2, 1, 3):
-                to_b(h, 4 - k, kb)
-            to_sib(h, 4 - k, 0)
-    for e in (0, 3, 1, 2):
-        for k in (1, 3, 2):
-            for h in (0, 1):
+                send(src, src, ag_send.at[h], ag_recv.at[h, 3 + 3 * (4 - k) + kb - 1], to_ab(h, 0, kb))
+    for h in (0, 1):
+        to_sib(h, 0)
+    for k in (1, 3, 2):
+        for h in (0, 1):
+            for e in (0, 3, 1, 2):
                 wait(xpart(h, e, 4 - k), ag_recv.at[h, 3 + 3 * e + k - 1])
-                to_sib(h, e, 4 - k)
+            to_sib(h, 4 - k)
     for h in (0, 1):
-        for da in range(4):
-            for db in range(4):
-                wait(xpart(h, da, db, 1), ag_recv.at[h, 15 + 4 * da + db])
-    for copy in local[2:]:
+        for db in (0, 3, 1, 2):
+            wait(xline(h, db, 1), ag_recv.at[h, 15 + db])
+    for copy in local[2:5]:
         copy.wait()
     table_copy.wait()
 
     def forward_pair(q, carry):
         a = jnp.concatenate([av[table[F_IDX, 2 * q]], av[table[F_IDX, 2 * q + 1]]], axis=1)
-        b = jnp.concatenate([xg[table[F_OTH, 2 * q]], xg[table[F_OTH, 2 * q + 1]]], axis=0)
+        halves_of = [(xa, F_OTH, 0), (xb, F_OTH_B, 0), (xa, F_OTH, 1), (xb, F_OTH_B, 1)]
+        b = jnp.concatenate([part[table[line, 2 * q + k]] for part, line, k in halves_of], axis=0)
         keep = table[F_KEEP, 2 * q].astype(F32)
-        total = acc[...] * keep + jnp.dot(a, b, preferred_element_type=F32)
-        acc[...] = total
+        total = carry * keep + jnp.dot(a, b, preferred_element_type=F32)
         fout[q] = total.astype(BF)
-        return carry
-
-    lax.fori_loop(0, FPAIRS, forward_pair, 0, unroll=4)
+        return total
+
+    lax.fori_loop(0, FPAIRS, forward_pair, jnp.zeros((TILE, F), F32), unroll=14)
 
     ROWS = TILE // Q
 
@@ -248,7 +249,6 @@
                     wait(gts[h].at[zat(1 - d, dist), part], zg_recv.at[d, dist - 1, q])
 
     gather_from(0, 0)
-    gather_from(0, 1)
     hv[...] = (pre * sig).astype(BF)
     hidden_copy = pltpu.make_async_copy(hv, hidden_o, out_sem.at[0])
     hidden_copy.start()
@@ -275,13 +275,12 @@
         total = w2s[x].astype(F32)
         for k in range(3):
             total = total + w2r[k].astype(F32)
-        w3s[0] = total[:, :128].astype(BF)
-        w3s[1] = total[:, 128:].astype(BF)
-        send(w3s.at[1 - core], w3r, w_send.at[2], w_recv.at[2], dev(flip=1))
+        w3s[...] = total.astype(BF)
+        send(w3s, w3r, w_send.at[2], w_recv.at[2], dev(flip=1))
 
     def w_stage4():
         wait(w3r, w_recv.at[2])
-        w4[zi] = (w3s[core].astype(F32) + w3r[...].astype(F32)).astype(BF)
+        w4[zi] = (w3s[...].astype(F32) + w3r[...].astype(F32)).astype(BF)
         for k in (1, 2, 3):
             send(w4.at[zi], w4.at[zi], w_send.at[3], w_recv.at[3], dev(zz=zq * 4 + (zi + k) % 4))
 
@@ -304,44 +303,37 @@
 
     def w_stage7():
         wait(w5.at[(zq + 2) % 4], w_recv.at[6])
-        w6[core] = sum4(w5)
-        send(w6.at[core], w6.at[core], w_send.at[6], w_recv.at[7], dev(flip=1))
-
-    def w_stage8():
-        wait(w6.at[1 - core], w_recv.at[7])
-        w7[x] = w6[...]
+        w7[x] = sum4(w5)
         for k in (1, 2, 3):
             send(w7.at[x], w7.at[x], w_send.at[7], w_recv.at[8], dev(dx=k))
 
-    def w_stage9():
+    def w_stage8():
         wait(w7.at[pl.ds(0, 3)], w_recv.at[8])
         w8[y] = w7[...]
         for k in (1, 2, 3):
             send(w8.at[y], w8.at[y], w_send.at[8], w_recv.at[9], dev(dy=k))
 
-    def w_stage10():
+    def w_stage9():
         wait(w8.at[pl.ds(0, 3)], w_recv.at[9])
         scale = (TILE * NX * NY * NZ * 2) ** -0.5
         for i in range(4):
             for j in range(4):
-                for k in range(2):
-                    gwv[pl.ds(64 * i + 16 * j, 16), pl.ds(128 * k, 128)] = w8[i, j, k].astype(F32) * scale
+                gwv[pl.ds(64 * i + 16 * j, 16), :] = w8[i, j].astype(F32) * scale
         gw_copy = pltpu.make_async_copy(gwv, gw_o, out_sem.at[1])
         gw_copy.start()
         return gw_copy
 
     w_stage1()
     gather_from(2, 0)
-    gather_from(2, 1)
+    gather_from(0, 1)
     w_stage2()
     gather_from(4, 0)
-    gather_from(4, 1)
+    gather_from(2, 1)
     w_stage3()
     gather_from(6, 0)
-    gather_from(6, 1)
+    gather_from(4, 1)
     w_stage4()
     gather_end(0)
-    w_stage5()
 
     def products(h, first, end):
         half = pl.ds(128 * h, 128)
@@ -350,14 +342,12 @@
             a = jnp.concatenate([gts[h][table[B_OTH, 2 * q]], gts[h][table[B_OTH, 2 * q + 1]]], axis=1)
             b = jnp.concatenate([av[table[B_IDX, 2 * q]], av[table[B_IDX, 2 * q + 1]]], axis=0)
             keep = table[B_KEEP, 2 * q].astype(F32)
-            total = gfv[half, :] * keep + jnp.dot(a, b, preferred_element_type=F32)
-            gfv[half, :] = total
+            total = carry * keep + jnp.dot(a, b, preferred_element_type=F32)
             bout[q, half, :] = total.astype(BF)
-            return carry
-
-        if first == 0:
-            gfv[half, :] = jnp.zeros((128, TILE), F32)
-        lax.fori_loop(first, end, backward_pair, 0, unroll=4)
+            return total
+
+        begin = jnp.zeros((128, TILE), F32) if first == 0 else gfv[half, :]
+        gfv[half, :] = lax.fori_loop(first, end, backward_pair, begin, unroll=16)
 
     def term(u, g, e, flip=0):
         dx, dy = (e, g) if u % 2 == 0 else (g, e)
@@ -409,33 +399,35 @@
             gft[pl.ds(64 * u, 64), :] = total
 
     MID = BPAIRS // 2
-    products(0, 0, BPAIRS)
+    products(0, 0, MID)
+    gather_from(6, 1)
+    w_stage5()
+    products(0, MID, BPAIRS)
     to_sibling(0)
-    w_stage6()
     gather_end(1)
     products(1, 0, MID)
     first_axis(0)
+    w_stage6()
     products(1, MID, BPAIRS)
     to_sibling(1)
+    first_axis(1)
     w_stage7()
-    first_axis(1)
+    second_axis(0)
+    second_axis(1)
     w_stage8()
-    second_axis(0)
-    w_stage9()
-    second_axis(1)
     last_sum(0)
-    gw_copy = w_stage10()
     last_sum(1)
-    hv2 = xg.at[NCOLS]
-    hv2[...] = jnp.transpose(gft[...]).astype(BF)
-    gf_copy = pltpu.make_async_copy(hv2, gf_o, out_sem.at[2])
+    gf_v[...] = jnp.transpose(gft[...]).astype(BF)
+    gf_copy = pltpu.make_async_copy(gf_v, gf_o, out_sem.at[2])
     gf_copy.start()
+    gw_copy = w_stage9()
     hidden_copy.wait()
     gw_copy.wait()
     gf_copy.wait()
-    wait(xg.at[pl.ds(0, NCOLS - 1)], ag_send)
-    wait(xg.at[pl.ds(0, NZ - 1)], zs_send)
-    wait(xg.at[pl.ds(0, NZ - 1)], zg_send)
+    for h in (0, 1):
+        wait(xs[h].at[pl.ds(0, NCOLS - 1)], ag_send.at[h])
+    wait(fout.at[pl.ds(0, NZ - 1)], zs_send)
+    wait(fout.at[pl.ds(0, NZ - 1)], zg_send)
     wait(sib_s, sb_send)
     wait(ps, rp_send.at[0])
     wait(qs, rp_send.at[1])
@@ -445,7 +437,6 @@
     wait(w4.at[pl.ds(0, 3)], w_send.at[3])
     wait(w5.at[pl.ds(0, 2)], w_send.at[4])
     wait(w5.at[0], w_send.at[5])
-    wait(w6.at[0], w_send.at[6])
     wait(w7.at[pl.ds(0, 3)], w_send.at[7])
     wait(w8.at[pl.ds(0, 3)], w_send.at[8])
 
@@ -469,12 +460,12 @@
         vm((1, 1, 1, SLOTS), jnp.int32),
         vm((1, 1, 1, SLOTS), jnp.int32),
         vm((8, 128), jnp.int32),
-        vm((8, 128), jnp.int32),
-        pltpu.SMEM((8, 128), jnp.int32),
+        vm((16, 128), jnp.int32),
+        pltpu.SMEM((16, 128), jnp.int32),
         vm((SLOTS, TILE, TILE), BF),
-        vm((NCOLS + 1, TILE, F), BF),
+        vm((NCOLS + 1, TILE // 2, F), BF),
+        vm((NCOLS + 1, TILE // 2, F), BF),
         vm((FPAIRS + 1, TILE, F), BF),
-        vm((TILE, F), F32),
         vm((F, F), BF),
         vm((TILE, F), BF),
         vm((2, 8, TILE, F), BF),
@@ -492,22 +483,22 @@
         vm((F, TILE), F32),
         vm((F, TILE), F32),
         vm((TILE, F), BF),
+        vm((TILE, F), BF),
         vm((4, 64, F), BF),
         vm((3, 64, F), BF),
         vm((4, 16, F), BF),
         vm((3, 16, F), BF),
-        vm((2, 16, 128), BF),
-        vm((16, 128), BF),
-        vm((4, 16, 128), BF),
-        vm((4, 16, 128), BF),
-        vm((2, 16, 128), BF),
-        vm((4, 2, 16, 128), BF),
-        vm((4, 4, 2, 16, 128), BF),
+        vm((16, F), BF),
+        vm((16, F), BF),
+        vm((4, 16, F), BF),
+        vm((4, 16, F), BF),
+        vm((4, 16, F), BF),
+        vm((4, 4, 16, F), BF),
         vm((F, F), F32),
         vm((F, F), F32),
         dma((8,)),
-        dma,
-        dma((2, 31)),
+        dma((2,)),
+        dma((2, 19)),
         dma,
         dma((2, 8, Q)),
         dma,

time: 93.7 us -> 88.2 us (0.941)
  Pallas kernels: 92.3 us -> 86.8 us
    pallas_call x1, Pallas kernels: 90.5 us -> 85 us  [per_device(): pl.pallas_call(kernel, out_shape=(jax.ShapeDtypeStruct((TILE, F), BF), ja...]
where the time goes in v4:
time: 88.2 us; the launch traced here: 88.1 us
  Pallas kernels  86.8 us (98%)
  between operations  1.29 us (1%)
    pallas_call x1, Pallas kernels, per_device(): pl.pallas_call(kernel, out_shape=(jax.ShapeDtypeStruct((TILE, F), BF), ja...  85 us
    pallas_call x1, Pallas kernels, per_device(): pl.pallas_call(hand_over, out_shape=[jax.ShapeDtypeStruct(a.shape, a.dtyp...  1.78 us

profile of v4, /device:TPU:1, one launch (start us, length us, event | category | flops | bytes accessed | tf_op | source)
XLA Modules:
  0.0 88.1 jit_solution(9796194645332248140)
XLA Ops:
  1.3 85.0 %shard_map.94 = (bf16[128,256]{1,0:T(8,128)(2,1)}, bf16[128,256]{1,0:T(8,128)(2,1)}, f32[256,256]{1,0:T(8,128)}) custom-call(s32[1,1,1]{2,1,0:T(1,128)S(6)} %copy.10.counts, s32[1,1,1,96]{3,2,1,0:T(1,128)} %rows_i.1, s32[1,1,1,96]{3,2,1,0:T(1,128)} %cols_i.1, bf16[128,256]{1,0:T(8,128)(2,1)} %feats.1, bf16[1,1,1,96,128,128]{5,4,3,2,1,0:T(8,128)(2,1)} %tiles.1, ...), custom_call_target="tpu_custom_call" | custom-call | flops 2000000000 | bytes 4000000 | tf_op jit(solution)/shard_map/pallas_call | solution.py:515
  86.3 1.8 %shard_map.95 = (bf16[128,256]{1,0:T(8,128)(2,1)}, bf16[128,256]{1,0:T(8,128)(2,1)}, f32[256,256]{1,0:T(8,128)}) custom-call(bf16[128,256]{1,0:T(8,128)(2,1)} %get-tuple-element.6.a, bf16[128,256]{1,0:T(8,128)(2,1)} %get-tuple-element.7.b, f32[256,256]{1,0:T(8,128)} %get-tuple-element.8.c), custom_call_target="tpu_custom_call" | custom-call | bytes 800000 | tf_op jit(solution)/shard_map/pallas_call | solution.py:530

commit v5 on v4

--- a/solution.py
+++ b/solution.py
@@ -13,7 +13,7 @@
 NROWS, NCOLS = NZ, NX * NY * 2
 FPOS, BPOS = SLOTS + NROWS, SLOTS + NCOLS
 FPAIRS, BPAIRS = FPOS // 2, BPOS // 2
-Q = 2
+Q = 4
 REL = (2, 1, 3, 0)
 
 F_IDX, F_OTH, F_KEEP, F_LAST, B_IDX, B_OTH, B_KEEP, B_LAST, F_OTH_B = range(9)

time: 88.2 us -> 87.2 us (0.989)
  Pallas kernels: 86.8 us -> 85.8 us
    pallas_call x1, Pallas kernels: 85 us -> 84 us  [per_device(): pl.pallas_call(kernel, out_shape=(jax.ShapeDtypeStruct((TILE, F), BF), ja...]
where the time goes in v5:
time: 87.2 us; the launch traced here: 87.1 us
  Pallas kernels  85.8 us (98%)
  between operations  1.29 us (1%)
    pallas_call x1, Pallas kernels, per_device(): pl.pallas_call(kernel, out_shape=(jax.ShapeDtypeStruct((TILE, F), BF), ja...  84 us
    pallas_call x1, Pallas kernels, per_device(): pl.pallas_call(hand_over, out_shape=[jax.ShapeDtypeStruct(a.shape, a.dtyp...  1.78 us

profile of v5, /device:TPU:1, one launch (start us, length us, event | category | flops | bytes accessed | tf_op | source)
XLA Modules:
  0.0 87.1 jit_solution(12783241191768874151)
XLA Ops:
  1.3 84.0 %shard_map.94 = (bf16[128,256]{1,0:T(8,128)(2,1)}, bf16[128,256]{1,0:T(8,128)(2,1)}, f32[256,256]{1,0:T(8,128)}) custom-call(s32[1,1,1]{2,1,0:T(1,128)S(6)} %copy.10.counts, s32[1,1,1,96]{3,2,1,0:T(1,128)} %rows_i.1, s32[1,1,1,96]{3,2,1,0:T(1,128)} %cols_i.1, bf16[128,256]{1,0:T(8,128)(2,1)} %feats.1, bf16[1,1,1,96,128,128]{5,4,3,2,1,0:T(8,128)(2,1)} %tiles.1, ...), custom_call_target="tpu_custom_call" | custom-call | flops 2000000000 | bytes 4000000 | tf_op jit(solution)/shard_map/pallas_call | solution.py:515
  85.3 1.8 %shard_map.95 = (bf16[128,256]{1,0:T(8,128)(2,1)}, bf16[128,256]{1,0:T(8,128)(2,1)}, f32[256,256]{1,0:T(8,128)}) custom-call(bf16[128,256]{1,0:T(8,128)(2,1)} %get-tuple-element.6.a, bf16[128,256]{1,0:T(8,128)(2,1)} %get-tuple-element.7.b, f32[256,256]{1,0:T(8,128)} %get-tuple-element.8.c), custom_call_target="tpu_custom_call" | custom-call | bytes 800000 | tf_op jit(solution)/shard_map/pallas_call | solution.py:530
